TPU v7x, 512 devices: a whole 4x8x8 slice. The times are simulated.
512 devices in a mesh: grad: 16 (over z, core), flow: 8 (over y_hi, x), vort: 4 (over y_lo).
Axes of the slice: x: 4, y: 8 (y_hi: 2, y_lo: 4; y = y_hi * 4 + y_lo), z: 8, core: 2. Of those that a mesh axis runs over, the one named last changes fastest.
Arguments:
- populations: float32 [19, 128, 128, 512], P(None, 'grad', 'flow', 'vort'), as said below
- thermal_noise: bfloat16 [15, 128, 128, 512], P(None, 'grad', 'flow', 'vort'), may hold values from -4 to 4
- relax_rates: float32 [15], replicated, may hold values from 0.4 to 1.8
- plane_shift: int32 [16], replicated, may hold values from 0 to 127
- fraction_index: int32 [1], replicated, may hold values from 1 to 7
- plane_speed: float32 [16], replicated, may hold values from 0.05 to 0.15
Outputs:
- read: float32 [19, 128, 128, 512], P(None, 'grad', 'flow', 'vort')
Inputs may be any that keep to these rules, and one draw needn't show every extreme that they name: `populations`: every value lies between 0.4 and 1.8. plane_shift[g] belongs to the plane between gradient slab g - 1 and slab g; plane 0 joins the last slab and the first.
All inputs are finite; a program needn't handle non-finite values.
Results may differ from a plain program's by a relative error of at most 0.0003.
Values sent between devices are 32-bit elements; how exact they have to be, the bound alone decides.
A program may use at most 64 MiB of HBM per device.

v0:
```python
import jax
import jax.numpy as jnp
import numpy as np
from jax import lax
from jax.sharding import PartitionSpec as P

FRACS = 8


THERMAL = 0.002


def with_halo(block, sides, width):
    for axis, dim in sides:
        count = lax.axis_size(axis)
        forward = [(i, i + 1) for i in range(count - 1)]
        forward.append((count - 1, 0))
        backward = [(target, source) for source, target in forward]
        low = lax.ppermute(
            lax.slice_in_dim(block, block.shape[dim] - width, None, axis=dim), axis, forward
        )
        high = lax.ppermute(lax.slice_in_dim(block, 0, width, axis=dim), axis, backward)
        block = jnp.concatenate([low, block, high], axis=dim)
    return block


def passed_along(x, axis, by):
    length = lax.axis_size(axis)
    return lax.ppermute(x, axis, [(i, (i + by) % length) for i in range(length)])


def lattice():
    velocity = (
        np.array(
            [
                [0, 0, 0],
                [1, 0, 0],
                [-1, 0, 0],
                [0, 1, 0],
                [0, -1, 0],
                [0, 0, 1],
                [0, 0, -1],
                [1, 1, 0],
                [-1, -1, 0],
                [1, -1, 0],
                [-1, 1, 0],
                [1, 0, 1],
                [-1, 0, -1],
                [1, 0, -1],
                [-1, 0, 1],
                [0, 1, 1],
                [0, -1, -1],
                [0, 1, -1],
                [0, -1, 1],
            ]
        )
        * 1.0
    )
    weights = np.array([1.0 / 3.0] + [1.0 / 18.0] * 6 + [1.0 / 36.0] * 12)
    axis_x = velocity[:, 0]
    axis_y = velocity[:, 1]
    axis_z = velocity[:, 2]
    monomials = [
        np.ones(19),
        axis_x,
        axis_y,
        axis_z,
        axis_x * axis_x,
        axis_y * axis_y,
        axis_z * axis_z,
        axis_x * axis_y,
        axis_x * axis_z,
        axis_y * axis_z,
        axis_x * axis_x * axis_y,
        axis_x * axis_x * axis_z,
        axis_y * axis_y * axis_x,
        axis_y * axis_y * axis_z,
        axis_z * axis_z * axis_x,
        axis_z * axis_z * axis_y,
        axis_x * axis_x * axis_y * axis_y,
        axis_x * axis_x * axis_z * axis_z,
        axis_y * axis_y * axis_z * axis_z,
    ]
    basis_list = []
    for monomial in monomials:
        vector = monomial.copy()
        for earlier in basis_list:
            vector = (
                vector
                - np.sum(weights * vector * earlier) / np.sum(weights * earlier * earlier) * earlier
            )
        basis_list.append(vector)
    mode_rows = np.stack(basis_list)
    mode_norms = np.sum(weights[None, :] * mode_rows * mode_rows, axis=1)
    return (velocity, weights, mode_rows, mode_norms)


def collide(flat_pops, flat_noise, relax_rates):
    velocity, weights, mode_rows, mode_norms = lattice()
    highest = lax.Precision.HIGHEST
    moment_table = jnp.asarray(
        np.concatenate([weights[None, :], weights[None, :] * velocity.T], 0), jnp.float32
    )
    totals = jnp.dot(moment_table, flat_pops, precision=highest)
    density = totals[0]
    mean_flow = totals[1:] / density[None, :]
    lattice_vel = jnp.asarray(velocity, jnp.float32)
    projected = jnp.dot(lattice_vel, mean_flow, precision=highest)
    speed_sq = jnp.sum(mean_flow * mean_flow, axis=0)
    equilibrium = density[None, :] * (
        1.0 + 3.0 * projected + 4.5 * projected * projected - 1.5 * speed_sq[None, :]
    )
    project_table = jnp.asarray(mode_rows[4:] * weights[None, :], jnp.float32)
    moments = jnp.dot(project_table, flat_pops - equilibrium, precision=highest)
    rate_col = relax_rates[:, None]
    norm_col = jnp.asarray(mode_norms[4:, None], jnp.float32)
    amplitude = jnp.sqrt(THERMAL * density[None, :] * norm_col * rate_col * (2.0 - rate_col))
    relaxed = (1.0 - rate_col) * moments + amplitude * flat_noise.astype(jnp.float32)
    expand_table = jnp.asarray((mode_rows[4:] / mode_norms[4:, None]).T, jnp.float32)
    return (equilibrium + jnp.dot(expand_table, relaxed, precision=highest), density, mean_flow)


def jump_row(direction, dens, flow, amount):
    step_x = float(direction[0])
    step_y = float(direction[1])
    step_z = float(direction[2])
    proj = step_x * flow[0] + step_y * flow[1] + step_z * flow[2]
    return dens * (
        3.0 * step_x * amount
        + 9.0 * proj * step_x * amount
        + 4.5 * step_x * step_x * amount * amount
        - 3.0 * flow[0] * amount
        - 1.5 * amount * amount
    )


def on_device(populations, thermal_noise, relax_rates, plane_shift, fraction_index, plane_speed):
    block_shape = populations.shape
    count_y = block_shape[1]
    count_x = block_shape[2]
    count_z = block_shape[3]
    velocity = lattice()[0]
    steps_x = [int(velocity[pop, 0]) for pop in range(19)]
    steps_y = [int(velocity[pop, 1]) for pop in range(19)]
    steps_z = [int(velocity[pop, 2]) for pop in range(19)]
    grad_index = lax.axis_index("grad")
    grad_count = lax.axis_size("grad")
    flow_index = lax.axis_index("flow")
    flat_collided, density, mean_flow = collide(
        populations.reshape(19, -1), thermal_noise.reshape(15, -1), relax_rates
    )
    collided = flat_collided.reshape(block_shape)
    dens_block = density.reshape(count_y, count_x, count_z)
    flow_block = mean_flow.reshape(3, count_y, count_x, count_z)
    amount_up = -plane_speed[(grad_index + 1) % grad_count]
    amount_down = plane_speed[grad_index]
    jumped_list = []
    for pop in range(19):
        if steps_y[pop] == 1:
            jumped_list.append(
                collided[pop]
                .at[count_y - 1]
                .add(
                    jump_row(
                        velocity[pop],
                        dens_block[count_y - 1],
                        flow_block[:, count_y - 1],
                        amount_up,
                    )
                )
            )
        elif steps_y[pop] == -1:
            jumped_list.append(
                collided[pop]
                .at[0]
                .add(jump_row(velocity[pop], dens_block[0], flow_block[:, 0], amount_down))
            )
        else:
            jumped_list.append(collided[pop])
    jumped = jnp.stack(jumped_list)
    padded = with_halo(jumped, (("flow", 2), ("vort", 3)), 1)
    moved = [
        padded[
            pop,
            :,
            1 - steps_x[pop] : 1 - steps_x[pop] + count_x,
            1 - steps_z[pop] : 1 - steps_z[pop] + count_z,
        ]
        for pop in range(19)
    ]
    up_ids = [pop for pop in range(19) if steps_y[pop] == 1]
    down_ids = [pop for pop in range(19) if steps_y[pop] == -1]
    top_rows = jnp.stack([moved[pop][count_y - 1] for pop in up_ids])
    bottom_rows = jnp.stack([moved[pop][0] for pop in down_ids])
    whole_top, whole_bottom = (
        lax.all_gather(top_rows, "flow", axis=1, tiled=True),
        lax.all_gather(bottom_rows, "flow", axis=1, tiled=True),
    )
    from_below = passed_along(whole_top, "grad", 1)
    from_above = passed_along(whole_bottom, "grad", -1)
    total_x = from_below.shape[1]
    shift_up = plane_shift[grad_index]
    shift_down = plane_shift[(grad_index + 1) % grad_count]
    weight_far = fraction_index[0].astype(jnp.float32) / FRACS
    doubled_below = jnp.concatenate([from_below, from_below], axis=1)
    begin_up = ((flow_index * count_x - shift_up - 1) % total_x).astype(jnp.int32)
    window_up = lax.dynamic_slice_in_dim(doubled_below, begin_up, count_x + 1, 1)
    lower_rows = (1.0 - weight_far) * window_up[:, 1:] + weight_far * window_up[:, :-1]
    doubled_above = jnp.concatenate([from_above, from_above], axis=1)
    begin_down = ((flow_index * count_x + shift_down) % total_x).astype(jnp.int32)
    window_down = lax.dynamic_slice_in_dim(doubled_above, begin_down, count_x + 1, 1)
    upper_rows = (1.0 - weight_far) * window_down[:, :-1] + weight_far * window_down[:, 1:]
    result = []
    for pop in range(19):
        if steps_y[pop] == 1:
            slot = up_ids.index(pop)
            result.append(jnp.concatenate([lower_rows[slot][None], moved[pop][:-1]], axis=0))
        elif steps_y[pop] == -1:
            slot = down_ids.index(pop)
            result.append(jnp.concatenate([moved[pop][1:], upper_rows[slot][None]], axis=0))
        else:
            result.append(moved[pop])
    return jnp.stack(result)


def solution(mesh):
    return jax.shard_map(
        on_device,
        mesh=mesh,
        in_specs=(
            P(None, "grad", "flow", "vort"),
            P(None, "grad", "flow", "vort"),
            P(),
            P(),
            P(),
            P(),
        ),
        out_specs=P(None, "grad", "flow", "vort"),
        check_vma=False,
    )
```

profile of v0, /device:TPU:199, one launch (start us, length us, event | category | flops | bytes accessed | tf_op | source)
XLA Modules:
  0.0 176.9 jit_solution(5475004786925660932)
XLA Ops:
  0.0 1.5 pad.135
  1.5 0.0 copy-start.7
  1.5 0.9 copy.53
  2.4 0.9 fusion.28
  3.4 0.1 broadcast_multiply_fusion
  3.5 0.2 fusion.16
  3.7 0.1 pad.136
  3.9 0.0 copy-start.10
  3.9 0.6 copy.54
  4.5 0.0 copy-done.8
  4.5 0.1 copy-done.10
  4.6 1.6 fusion.4
  6.3 1.7 fusion.1
  8.0 1.4 convolution_add_fusion
  9.4 1.1 fusion.21
  10.5 0.1 fusion.20
  10.7 0.7 fusion.27
  16.7 1.0 copy.84
  19.8 0.6 constant_dynamic-update-slice_fusion.28
  20.8 0.1 fusion.22
  20.9 7.4 %collective-permute-start = (f32[19,8,1,128]{3,2,1,0:T(1,128)S(1)}, f32[19,8,1,128]{3,2,1,0:T(1,128)S(1)}, u32[]{:S(2)}, u32[]{:S(2)}) collective-permute-start(f32[19,8,1,128]{3,2,1,0:T(1,128)S(1)} %get-tuple-element.175), channel_id=1, source_target_pairs={{0,4},{4,8},{8,12},{12,16},{16,20},{20,24},{24,28},{28,0},{1,5},{5... | collective-permute-start | bytes 233480 | tf_op jit(solution)/shard_map/ppermute | solution.py:19
  28.3 1.9 %collective-permute-start.1 = (f32[19,8,1,128]{3,2,1,0:T(1,128)S(1)}, f32[19,8,1,128]{3,2,1,0:T(1,128)S(1)}, u32[]{:S(2)}, u32[]{:S(2)}) collective-permute-start(f32[19,8,1,128]{3,2,1,0:T(1,128)S(1)} %get-tuple-element.174), channel_id=1, source_target_pairs={{4,0},{8,4},{12,8},{16,12},{20,16},{24,20},{28,24},{0,28},{5,1},{9... | collective-permute-start | bytes 233480 | tf_op jit(solution)/shard_map/ppermute | solution.py:22
  30.2 0.7 fusion.26
  33.0 6.6 %collective-permute-done.1 = f32[19,8,1,128]{3,2,1,0:T(1,128)S(1)} collective-permute-done((f32[19,8,1,128]{3,2,1,0:T(1,128)S(1)}, f32[19,8,1,128]{3,2,1,0:T(1,128)S(1)}, u32[]{:S(2)}, u32[]{:S(2)}) %collective-permute-start.1) | collective-permute-done | bytes 77856 | tf_op jit(solution)/shard_map/ppermute | solution.py:22
  39.5 0.3 pad_maximum_fusion
  39.9 2.4 %fusion.19 = (f32[19,8,18,1]{3,2,1,0:T(8,128)}, f32[19,8,18,1]{3,2,1,0:T(8,128)}) fusion(f32[19,8,18,128]{3,2,1,0:T(8,128)S(1)} %pad_maximum_fusion), kind=kLoop, calls=%fused_computation.132 | loop fusion | bytes 43776 | tf_op jit(solution)/shard_map/slice | solution.py:22
  42.3 3.2 %copy.51 = f32[19,8,18,1]{0,1,3,2:T(8,128)} copy(f32[19,8,18,1]{3,2,1,0:T(8,128)} %get-tuple-element.135) | data formatting | bytes 21888 | tf_op jit(solution)/shard_map/slice | solution.py:22
  45.5 4.6 %collective-permute-start.3 = (f32[19,8,18,1]{0,1,3,2:T(8,128)}, f32[19,8,18,1]{0,1,3,2:T(8,128)}, u32[]{:S(2)}, u32[]{:S(2)}) collective-permute-start(f32[19,8,18,1]{0,1,3,2:T(8,128)} %copy.51), channel_id=1, source_target_pairs={{1,0},{2,1},{3,2},{0,3},{5,4},{6,5},{7,6},{4,7},{9,8},{10,9},{11,1... | collective-permute-start | bytes 32840 | tf_op jit(solution)/shard_map/ppermute | solution.py:22
  50.2 1.8 %copy.49 = f32[19,8,18,1]{0,1,3,2:T(8,128)} copy(f32[19,8,18,1]{3,2,1,0:T(8,128)S(1)} %copy-done.1) | data formatting | bytes 21888 | tf_op jit(solution)/shard_map/slice | solution.py:20
  52.0 1.9 %collective-permute-start.2 = (f32[19,8,18,1]{0,1,3,2:T(8,128)}, f32[19,8,18,1]{0,1,3,2:T(8,128)}, u32[]{:S(2)}, u32[]{:S(2)}) collective-permute-start(f32[19,8,18,1]{0,1,3,2:T(8,128)} %copy.49), channel_id=1, source_target_pairs={{0,1},{1,2},{2,3},{3,0},{4,5},{5,6},{6,7},{7,4},{8,9},{9,10},{10,1... | collective-permute-start | bytes 32840 | tf_op jit(solution)/shard_map/ppermute | solution.py:19
  53.9 0.6 constant_dynamic-update-slice_fusion.46
  54.6 0.6 constant_dynamic-update-slice_fusion.27
  55.2 0.6 constant_dynamic-update-slice_fusion.26
  55.8 2.9 %copy.52 = f32[19,8,18,1]{3,2,1,0:T(8,128)S(1)} copy(f32[19,8,18,1]{0,1,3,2:T(8,128)} %collective-permute-done.3) | data formatting | bytes 21888 | tf_op jit(solution)/shard_map/ppermute | solution.py:22
  58.6 0.5 collective-permute-done.2
  59.2 3.9 %copy.50 = f32[19,8,18,1]{3,2,1,0:T(8,128)} copy(f32[19,8,18,1]{0,1,3,2:T(8,128)} %collective-permute-done.2) | data formatting | bytes 21888 | tf_op jit(solution)/shard_map/ppermute | solution.py:19
  63.1 0.7 constant_dynamic-update-slice_fusion.25
  63.7 0.6 constant_dynamic-update-slice_fusion.21
  64.3 0.3 copy-done
  64.6 0.7 constant_dynamic-update-slice_fusion.24
  65.3 0.7 constant_dynamic-update-slice_fusion.19
  65.9 38.0 %all_gather.6 = f32[5,128,128]{2,1,0:T(8,128)S(1)} all-gather(f32[5,16,128]{2,1,0:T(8,128)} %constant_dynamic-update-slice_fusion.19), channel_id=1, replica_groups=mesh['grad'=16,'flow'=8,'vort'=4] {'flow'}, dimensions={1}, use_global_device_ids=true | all-gather | bytes 368640 | tf_op jit(solution)/shard_map/all_gather | solution.py:196
  103.9 12.1 %collective-permute-start.4 = (f32[5,128,128]{2,1,0:T(8,128)S(1)}, f32[5,128,128]{2,1,0:T(8,128)S(1)}, u32[]{:S(2)}, u32[]{:S(2)}) collective-permute-start(f32[5,128,128]{2,1,0:T(8,128)S(1)} %all_gather.6), channel_id=1, source_target_pairs={{0,32},{32,64},{64,96},{96,128},{128,160},{160,192},{192,224},{224... | collective-permute-start | bytes 983048 | tf_op jit(solution)/shard_map/ppermute | solution.py:29
  116.0 0.6 constant_dynamic-update-slice_fusion.45
  116.6 38.4 %all_gather.7 = f32[5,128,128]{2,1,0:T(8,128)S(1)} all-gather(f32[5,16,128]{2,1,0:T(8,128)} %get-tuple-element.133), channel_id=1, replica_groups=mesh['grad'=16,'flow'=8,'vort'=4] {'flow'}, dimensions={1}, use_global_device_ids=true | all-gather | bytes 368640 | tf_op jit(solution)/shard_map/all_gather | solution.py:197
  155.1 2.9 %collective-permute-start.5 = (f32[5,128,128]{2,1,0:T(8,128)S(1)}, f32[5,128,128]{2,1,0:T(8,128)S(1)}, u32[]{:S(2)}, u32[]{:S(2)}) collective-permute-start(f32[5,128,128]{2,1,0:T(8,128)S(1)} %all_gather.7), channel_id=1, source_target_pairs={{0,480},{32,0},{64,32},{96,64},{128,96},{160,128},{192,160},{224,1... | collective-permute-start | bytes 983048 | tf_op jit(solution)/shard_map/ppermute | solution.py:29
  158.0 0.2 fusion.8
  158.2 7.8 %collective-permute-done.5 = f32[5,128,128]{2,1,0:T(8,128)S(1)} collective-permute-done((f32[5,128,128]{2,1,0:T(8,128)S(1)}, f32[5,128,128]{2,1,0:T(8,128)S(1)}, u32[]{:S(2)}, u32[]{:S(2)}) %collective-permute-start.5) | collective-permute-done | bytes 327712 | tf_op jit(solution)/shard_map/ppermute | solution.py:29
  166.1 0.6 constant_dynamic-update-slice_fusion.44
  166.7 0.6 constant_dynamic-update-slice_fusion.43
  167.3 0.7 constant_dynamic-update-slice_fusion.42
  168.1 0.7 constant_dynamic-update-slice_fusion.41
  168.8 0.6 constant_dynamic-update-slice_fusion.40
  169.5 0.6 constant_dynamic-update-slice_fusion.39
  170.1 0.6 constant_dynamic-update-slice_fusion.38
  170.7 0.6 constant_dynamic-update-slice_fusion.37
  171.4 0.7 constant_dynamic-update-slice_fusion.36
  172.1 0.8 constant_dynamic-update-slice_fusion.35
  172.8 0.7 constant_dynamic-update-slice_fusion.34
  173.6 0.7 constant_dynamic-update-slice_fusion.33
  174.3 0.6 constant_dynamic-update-slice_fusion.32
  174.9 0.6 constant_dynamic-update-slice_fusion.31
  175.6 0.6 constant_dynamic-update-slice_fusion.30
  176.2 0.6 constant_dynamic-update-slice_fusion.29
  (57 shorter events, 0.4 us)
Async XLA Ops:
  1.5 0.9 copy-start.7
  2.4 1.3 copy-start.2
  3.9 0.7 copy-start.8
  3.9 0.7 copy-start.10
  4.6 1.7 copy-start.4
  4.6 1.7 copy-start.9
  6.3 1.7 copy-start.3
  9.4 1.2 copy-start.5
  20.5 9.7 %copy-start.6 = (s32[16]{0:T(128)S(1)}, s32[16]{0:T(128)}, u32[]{:S(2)}) copy-start(s32[16]{0:T(128)} %param.34) | copy-start | bytes 196
  20.9 12.1 %collective-permute-start = (f32[19,8,1,128]{3,2,1,0:T(1,128)S(1)}, f32[19,8,1,128]{3,2,1,0:T(1,128)S(1)}, u32[]{:S(2)}, u32[]{:S(2)}) collective-permute-start(f32[19,8,1,128]{3,2,1,0:T(1,128)S(1)} %get-tuple-element.175), channel_id=1, source_target_pairs={{0,4},{4,8},{8,12},{12,16},{16,20},{20,24},{24,28},{28,0},{1,5},{5... | collective-permute-start | bytes 233480 | tf_op jit(solution)/shard_map/ppermute | solution.py:19
  28.3 11.3 %collective-permute-start.1 = (f32[19,8,1,128]{3,2,1,0:T(1,128)S(1)}, f32[19,8,1,128]{3,2,1,0:T(1,128)S(1)}, u32[]{:S(2)}, u32[]{:S(2)}) collective-permute-start(f32[19,8,1,128]{3,2,1,0:T(1,128)S(1)} %get-tuple-element.174), channel_id=1, source_target_pairs={{4,0},{8,4},{12,8},{16,12},{20,16},{24,20},{28,24},{0,28},{5,1},{9... | collective-permute-start | bytes 233480 | tf_op jit(solution)/shard_map/ppermute | solution.py:22
  42.3 7.9 %copy-start.1 = (f32[19,8,18,1]{3,2,1,0:T(8,128)S(1)}, f32[19,8,18,1]{3,2,1,0:T(8,128)}, u32[]{:S(2)}) copy-start(f32[19,8,18,1]{3,2,1,0:T(8,128)} %get-tuple-element.136) | copy-start | bytes 32836
  45.5 10.2 %collective-permute-start.3 = (f32[19,8,18,1]{0,1,3,2:T(8,128)}, f32[19,8,18,1]{0,1,3,2:T(8,128)}, u32[]{:S(2)}, u32[]{:S(2)}) collective-permute-start(f32[19,8,18,1]{0,1,3,2:T(8,128)} %copy.51), channel_id=1, source_target_pairs={{1,0},{2,1},{3,2},{0,3},{5,4},{6,5},{7,6},{4,7},{9,8},{10,9},{11,1... | collective-permute-start | bytes 32840 | tf_op jit(solution)/shard_map/ppermute | solution.py:22
  52.0 7.2 %collective-permute-start.2 = (f32[19,8,18,1]{0,1,3,2:T(8,128)}, f32[19,8,18,1]{0,1,3,2:T(8,128)}, u32[]{:S(2)}, u32[]{:S(2)}) collective-permute-start(f32[19,8,18,1]{0,1,3,2:T(8,128)} %copy.49), channel_id=1, source_target_pairs={{0,1},{1,2},{2,3},{3,0},{4,5},{5,6},{6,7},{7,4},{8,9},{9,10},{10,1... | collective-permute-start | bytes 32840 | tf_op jit(solution)/shard_map/ppermute | solution.py:19
  63.1 1.5 copy-start
  103.9 54.3 %collective-permute-start.4 = (f32[5,128,128]{2,1,0:T(8,128)S(1)}, f32[5,128,128]{2,1,0:T(8,128)S(1)}, u32[]{:S(2)}, u32[]{:S(2)}) collective-permute-start(f32[5,128,128]{2,1,0:T(8,128)S(1)} %all_gather.6), channel_id=1, source_target_pairs={{0,32},{32,64},{64,96},{96,128},{128,160},{160,192},{192,224},{224... | collective-permute-start | bytes 983048 | tf_op jit(solution)/shard_map/ppermute | solution.py:29
  155.1 10.9 %collective-permute-start.5 = (f32[5,128,128]{2,1,0:T(8,128)S(1)}, f32[5,128,128]{2,1,0:T(8,128)S(1)}, u32[]{:S(2)}, u32[]{:S(2)}) collective-permute-start(f32[5,128,128]{2,1,0:T(8,128)S(1)} %all_gather.7), channel_id=1, source_target_pairs={{0,480},{32,0},{64,32},{96,64},{128,96},{160,128},{192,160},{224,1... | collective-permute-start | bytes 983048 | tf_op jit(solution)/shard_map/ppermute | solution.py:29
where the time goes:
time: 177 us
  blocking collectives  76.4 us (43%)
  starting transfers between devices  30.8 us (17%)
  local copies, waits for them, and re-layouts  21.5 us (12%)
  other arithmetic  17.5 us (10%)
  waiting for transfers between devices  14.9 us (8%)
  between operations  10 us (6%)
  matrix products  5.72 us (3%)
    all_gather x1, blocking collectives, on_device(): lax.all_gather(bottom_rows, 'flow', axis=1, tiled=True)  38.4 us
    all_gather x1, blocking collectives, on_device(): lax.all_gather(top_rows, 'flow', axis=1, tiled=True)  38 us
    ppermute x2, starting transfers between devices, passed_along(): lax.ppermute(x, axis, [(i, (i + by) % length) for i in range(length)])  15 us
    unnamed x23, other arithmetic  14.7 us
    ppermute x2, starting transfers between devices, with_halo(): lax.ppermute(lax.slice_in_dim(block, block.shape[dim] - width, None, axis...  9.28 us
    ppermute x2, waiting for transfers between devices, passed_along(): lax.ppermute(x, axis, [(i, (i + by) % length) for i in range(length)])  7.77 us
    ppermute x2, waiting for transfers between devices, with_halo(): lax.ppermute(lax.slice_in_dim(block, 0, width, axis=dim), axis, backward)  6.57 us
    ppermute x2, starting transfers between devices, with_halo(): lax.ppermute(lax.slice_in_dim(block, 0, width, axis=dim), axis, backward)  6.56 us
  transfers between devices with their start and end apart: 6, of which 3 were waited for; matrix products, arithmetic and copies ran while one was open for 5% of the time, Pallas kernels for 0%

commit v1 on v0

v1 whole, which is shorter than its diff:
```python
import functools

import jax
import jax.numpy as jnp
import numpy as np
from jax import lax
from jax.experimental import pallas as pl
from jax.experimental.pallas import tpu as pltpu
from jax.sharding import PartitionSpec as P

FRACS = 8
THERMAL = 0.002
MESH = pl.DeviceIdType.MESH

FLOW_UP = (1, 7, 9, 11, 13)
FLOW_DOWN = (2, 8, 10, 12, 14)
FLOW_STAY = (0, 3, 4, 5, 6, 15, 16, 17, 18)
CROSS_UP = (3, 7, 10, 15, 17)
CROSS_DOWN = (4, 8, 9, 18, 16)
VORT_UP = (5, 11, 14, 15, 18)
VORT_DOWN = (6, 12, 13, 16, 17)


def lattice():
    axes = [[1, 0, 0], [0, 1, 0], [0, 0, 1]]
    edges = [[1, 1, 0], [1, -1, 0], [1, 0, 1], [1, 0, -1], [0, 1, 1], [0, 1, -1]]
    rows = [[0, 0, 0]]
    for step in axes + edges:
        rows += [step, [-part for part in step]]
    velocity = np.array(rows) * 1.0
    weights = np.array([1.0 / 3.0] + [1.0 / 18.0] * 6 + [1.0 / 36.0] * 12)
    x, y, z = velocity.T
    monomials = [np.ones(19), x, y, z, x * x, y * y, z * z, x * y, x * z, y * z]
    monomials += [x * x * y, x * x * z, y * y * x, y * y * z, z * z * x, z * z * y]
    monomials += [x * x * y * y, x * x * z * z, y * y * z * z]
    basis = []
    for monomial in monomials:
        vector = monomial.copy()
        for earlier in basis:
            vector = vector - np.sum(weights * vector * earlier) / np.sum(weights * earlier * earlier) * earlier
        basis.append(vector)
    modes = np.stack(basis)
    return velocity, weights, modes, np.sum(weights[None, :] * modes * modes, axis=1)


VELOCITY, WEIGHTS, MODES, NORMS = lattice()
STEPS = VELOCITY.astype(int)
PAIRS = [(i, i + 1) for i in range(1, 19, 2)]
ODD = (1, 2, 3, 10, 11, 12, 13, 14, 15)
EVEN = (0, 4, 5, 6, 7, 8, 9, 16, 17, 18)


def combine(factors, values):
    groups = {}
    for factor, value in zip(factors, values):
        if abs(factor) > 1e-9:
            groups.setdefault(round(abs(float(factor)), 9), []).append((factor, value))
    total = None
    for members in groups.values():
        members.sort(key=lambda member: member[0] < 0)
        lead, part = members[0]
        for factor, value in members[1:]:
            part = part + value if (factor > 0) == (lead > 0) else part - value
        size = abs(float(lead))
        if abs(size - 1.0) > 1e-9:
            part = part * size
        if total is None:
            total = part if lead > 0 else -part
        else:
            total = total + part if lead > 0 else total - part
    return total


def collide(pops, noise, rates, spread):
    sums = [pops[0]] + [pops[a] + pops[b] for a, b in PAIRS]
    gaps = [pops[a] - pops[b] for a, b in PAIRS]
    ids = [0] + [a for a, _ in PAIRS]
    table = MODES * WEIGHTS[None, :]
    moments = {}
    for k in EVEN:
        moments[k] = combine([table[k, i] for i in ids], sums)
    for k in ODD:
        moments[k] = combine([table[k, i] for i in ids[1:]], gaps)
    density = moments[0]
    inverse = 1.0 / density
    flow = [moments[1] * inverse, moments[2] * inverse, moments[3] * inverse]
    root = jnp.sqrt(density)
    second = {}
    for k, (a, b) in zip(range(4, 10), ((0, 0), (1, 1), (2, 2), (0, 1), (0, 2), (1, 2))):
        second[(a, b)] = moments[1 + a] * flow[b]
    scaled = {k: moments[k] * (1.0 / NORMS[k]) for k in range(4)}
    for k in range(4, 19):
        at_rest = None
        if k < 10:
            at_rest = equilibrium_moment(k, second)
        excess = moments[k] if at_rest is None else moments[k] - at_rest
        relaxed = (1.0 - rates[k - 4]) * excess + root * spread(k - 4) * noise(k - 4)
        if at_rest is not None:
            relaxed = relaxed + at_rest
        scaled[k] = relaxed * (1.0 / NORMS[k])
    collided = [None] * 19
    even = [combine([MODES[k, i] for k in EVEN], [scaled[k] for k in EVEN]) for i in ids]
    odd = [combine([MODES[k, i] for k in ODD], [scaled[k] for k in ODD]) for i in ids[1:]]
    collided[0] = even[0]
    for slot, (a, b) in enumerate(PAIRS):
        collided[a] = even[slot + 1] + odd[slot]
        collided[b] = even[slot + 1] - odd[slot]
    return collided, density, flow


def equilibrium_moment(k, second):
    pairs = [(0, 0), (1, 1), (2, 2), (0, 1), (0, 2), (1, 2)]
    factors = []
    for a, b in pairs:
        factor = 4.5 * np.sum(MODES[k] * WEIGHTS * VELOCITY[:, a] * VELOCITY[:, b])
        factors.append(factor if a == b else 2.0 * factor)
    return combine(factors, [second[pair] for pair in pairs])


def jump(pop, density, flow, amount):
    step_x, step_y, step_z = (float(part) for part in STEPS[pop])
    projected = combine((step_x, step_y, step_z), flow)
    inside = -3.0 * amount * flow[0] + (3.0 * step_x * amount - 1.5 * amount * amount)
    if step_x:
        inside = inside + (9.0 * step_x * amount) * projected + 4.5 * amount * amount
    return density * inside


def kernel(
    pop_hbm, noise_hbm, rates_hbm, shift_hbm, frac_hbm, speed_hbm, out,
    pv, nv, rates, shift, frac, speed, spread_ref, upad, dpad, stay,
    send_up, send_down, first_up, first_down, edge_up, edge_down,
    next_up, next_down, window_up, window_down,
    flow_out, flow_in, vort_out, vort_in, square,
    load_sem, send_sem, recv_sem,
):
    g, f, v = lax.axis_index("grad"), lax.axis_index("flow"), lax.axis_index("vort")
    grads, flows, vorts = lax.axis_size("grad"), lax.axis_size("flow"), lax.axis_size("vort")
    half = flows // 2
    side, x = f // half, f % half
    rows = pv.shape[1]

    def place(by_g, by_side, by_x, by_v):
        flow_at = lax.rem(side + by_side, 2) * half + lax.rem(x + by_x + half, half)
        return (lax.rem(g + by_g + grads, grads), flow_at, lax.rem(v + by_v + vorts, vorts))

    def along(by_f):
        return (g, lax.rem(f + by_f + flows, flows), v)

    loads = []

    def load(source, target):
        loads.append(pltpu.make_async_copy(source, target, load_sem.at[len(loads)]))
        loads[-1].start()

    load(pop_hbm.at[:, rows - 1], pv.at[:, rows - 1])
    load(noise_hbm.at[:, rows - 1], nv.at[:, rows - 1])
    load(rates_hbm, rates)
    load(speed_hbm, speed)
    load(pop_hbm.at[:, 0], pv.at[:, 0])
    load(noise_hbm.at[:, 0], nv.at[:, 0])
    load(shift_hbm, shift)
    load(frac_hbm, frac)
    load(pop_hbm.at[:, pl.ds(1, rows - 2)], pv.at[:, pl.ds(1, rows - 2)])
    load(noise_hbm.at[:, pl.ds(1, rows - 2)], nv.at[:, pl.ds(1, rows - 2)])

    partners = [along(1), along(-1), place(0, 0, 0, 1), place(0, 0, 0, -1)]
    partners += [place(0, 0, step, 0) for step in (1, 2, 3)]
    partners += [place(a, b, 0, c) for a in (1, -1) for b in (0, 1) for c in (0, 1, -1)]
    barrier = pltpu.get_barrier_semaphore()
    for partner in partners:
        pl.semaphore_signal(barrier, inc=1, device_id=partner, device_id_type=MESH)

    copies = []

    def send(source, target, device):
        number = len(copies)
        copies.append(
            pltpu.make_async_remote_copy(
                src_ref=source,
                dst_ref=target,
                send_sem=send_sem.at[number],
                recv_sem=recv_sem.at[number],
                device_id=device,
                device_id_type=MESH,
            )
        )
        copies[-1].start()
        return copies[-1]

    lane = lax.broadcasted_iota(jnp.int32, (16, 128), 1)

    def collide_row(y):
        pops = [pv[i, y] for i in range(19)]
        return collide(
            pops,
            lambda k: nv[k, y].astype(jnp.float32),
            [rates[k] for k in range(15)],
            lambda k: jnp.concatenate([spread_ref[k], spread_ref[k]], axis=0),
        )

    def keep(y, collided):
        for slot, pop in enumerate(FLOW_UP):
            upad[slot, y, 8:24, :] = collided[pop]
        for slot, pop in enumerate(FLOW_DOWN):
            dpad[slot, y, 0:16, :] = collided[pop]
        for slot, pop in enumerate(FLOW_STAY):
            stay[slot, y] = collided[pop]

    def first_stage(by_g, rows_out, first, edge):
        return [
            send(rows_out, first.at[1], place(by_g, 1, 0, 0)),
            send(rows_out.at[3], edge.at[1, 0], place(by_g, 1, 0, 1)),
            send(rows_out.at[4], edge.at[1, 1], place(by_g, 1, 0, -1)),
            send(rows_out, first.at[0], place(by_g, 0, 0, 0)),
            send(rows_out.at[3], edge.at[0, 0], place(by_g, 0, 0, 1)),
            send(rows_out.at[4], edge.at[0, 1], place(by_g, 0, 0, -1)),
        ]

    for copy in loads[:4]:
        copy.wait()
    for k in range(15):
        scale = THERMAL * float(NORMS[k + 4]) * rates[k] * (2.0 - rates[k])
        spread_ref[k] = jnp.sqrt(jnp.full((8, 128), scale, jnp.float32))
    collided, density, flow = collide_row(rows - 1)
    amount = -speed[lax.rem(g + 1, grads)]
    for slot, pop in enumerate(CROSS_UP):
        send_up[slot] = collided[pop] + jump(pop, density, flow, amount)
    pl.semaphore_wait(barrier, len(partners))
    up_first = first_stage(1, send_up, first_up, edge_up)
    keep(rows - 1, collided)

    for copy in loads[4:8]:
        copy.wait()
    collided, density, flow = collide_row(0)
    amount = speed[g]
    for slot, pop in enumerate(CROSS_DOWN):
        send_down[slot] = collided[pop] + jump(pop, density, flow, amount)
    down_first = first_stage(-1, send_down, first_down, edge_down)
    keep(0, collided)

    for copy in loads[8:]:
        copy.wait()

    def middle(y, carry):
        keep(y, collide_row(y)[0])
        return carry

    lax.fori_loop(1, rows - 1, middle, 0)

    for slot in range(5):
        for y in range(rows):
            flow_out[0, slot, y : y + 1, :] = upad[slot, y, 23:24, :]
            flow_out[1, slot, y : y + 1, :] = dpad[slot, y, 0:1, :]
    flow_halo = [
        send(flow_out.at[0], flow_in.at[0], along(1)),
        send(flow_out.at[1], flow_in.at[1], along(-1)),
    ]
    for copy in flow_halo:
        copy.wait_recv()
    for slot in range(5):
        for y in range(rows):
            upad[slot, y, 7:8, :] = flow_in[0, slot, y : y + 1, :]
            dpad[slot, y, 16:17, :] = flow_in[1, slot, y : y + 1, :]

    def shifted(pop, y):
        if pop in FLOW_UP:
            return upad[FLOW_UP.index(pop), y, 7:23, :]
        if pop in FLOW_DOWN:
            return dpad[FLOW_DOWN.index(pop), y, 1:17, :]
        return stay[FLOW_STAY.index(pop), y]

    for y in range(rows):
        tile = jnp.zeros((16, 128), jnp.float32)
        for slot, pop in enumerate(VORT_UP):
            tile = jnp.where(lane == slot, pltpu.roll(shifted(pop, y), slot + 1, 1), tile)
        for slot, pop in enumerate(VORT_DOWN):
            tile = jnp.where(lane == 8 + slot, pltpu.roll(shifted(pop, y), 8 + slot, 1), tile)
        square[16 * y : 16 * y + 16, :] = tile
    vort_out[...] = square[...].T[0:16, :]
    vort_halo = [
        send(vort_out.at[pl.ds(0, 8)], vort_in.at[pl.ds(0, 8)], place(0, 0, 0, 1)),
        send(vort_out.at[pl.ds(8, 8)], vort_in.at[pl.ds(8, 8)], place(0, 0, 0, -1)),
    ]

    def target_rows(pop):
        step = int(STEPS[pop, 1])
        return [(y, y + step) for y in range(rows) if 0 <= y + step < rows]

    for pop in range(19):
        if STEPS[pop, 2] == 0:
            for y, to in target_rows(pop):
                out[pop, to] = shifted(pop, y)

    for copy in vort_halo:
        copy.wait_recv()
    square[...] = jnp.concatenate([vort_in[...], jnp.zeros((112, 128), jnp.float32)], axis=0).T
    for slot, (up, down) in enumerate(zip(VORT_UP, VORT_DOWN)):
        for y, to in target_rows(up):
            edge = pltpu.roll(square[16 * y : 16 * y + 16, :], (128 - slot) % 128, 1)
            out[up, to] = jnp.where(lane == 0, edge, pltpu.roll(shifted(up, y), 1, 1))
        for y, to in target_rows(down):
            edge = pltpu.roll(square[16 * y : 16 * y + 16, :], 119 - slot, 1)
            out[down, to] = jnp.where(lane == 127, edge, pltpu.roll(shifted(down, y), 127, 1))

    far = frac[0].astype(jnp.float32) * (1.0 / FRACS)

    def second_stage(arrived, first, edge, onward, window, crossing, offset, sign):
        for copy in arrived:
            copy.wait_recv()
        for which in range(2):
            first[which, 3] = pltpu.roll(jnp.where(lane == 127, edge[which, 0], first[which, 3]), 1, 1)
            first[which, 4] = pltpu.roll(jnp.where(lane == 0, edge[which, 1], first[which, 4]), 127, 1)
        sent = []
        for step in (2, 1, 3, 0):
            to_x = lax.rem(x + sign * step + half, half)
            apart = sign * (to_x - x)
            for slot, pop in enumerate(crossing):
                moved = offset + sign * int(STEPS[pop, 0])
                chosen = ((apart - ((moved & 127) >> 4)) & 7) >> 2
                block = first[chosen, slot]
                if step:
                    onward[step - 1, slot] = block
                else:
                    window[slot, 0:16, :] = block
                    window[slot, 64:80, :] = block
            if step:
                begin = 64 - 16 * step if sign > 0 else 16 * step
                sent.append(
                    send(onward.at[step - 1], window.at[:, pl.ds(begin, 16)], place(0, 0, sign * step, 0))
                )
        return sent

    def finish(arrived, window, crossing, offset, sign, to):
        for copy in arrived:
            copy.wait_recv()
        for slot, pop in enumerate(crossing):
            moved = (offset + sign * int(STEPS[pop, 0])) & 63
            begin = 64 - moved if sign > 0 else moved
            near_part = window[slot, pl.ds(begin, 16), :]
            far_part = window[slot, pl.ds(begin - sign, 16), :]
            out[pop, to] = (1.0 - far) * near_part + far * far_part

    down_offset, up_offset = shift[lax.rem(g + 1, grads)], shift[g]
    down_next = second_stage(down_first, first_down, edge_down, next_down, window_down, CROSS_DOWN, down_offset, -1)
    finish(down_next, window_down, CROSS_DOWN, down_offset, -1, rows - 1)
    up_next = second_stage(up_first, first_up, edge_up, next_up, window_up, CROSS_UP, up_offset, 1)
    finish(up_next, window_up, CROSS_UP, up_offset, 1, 0)
    for copy in copies:
        copy.wait_send()


def on_device(populations, thermal_noise, relax_rates, plane_shift, fraction_index, plane_speed):
    rows = populations.shape[1]
    scratch = [
        pltpu.VMEM(populations.shape, jnp.float32),
        pltpu.VMEM(thermal_noise.shape, jnp.bfloat16),
        pltpu.SMEM(relax_rates.shape, jnp.float32),
        pltpu.SMEM(plane_shift.shape, jnp.int32),
        pltpu.SMEM(fraction_index.shape, jnp.int32),
        pltpu.SMEM(plane_speed.shape, jnp.float32),
        pltpu.VMEM((15, 8, 128), jnp.float32),
        pltpu.VMEM((5, rows, 24, 128), jnp.float32),
        pltpu.VMEM((5, rows, 24, 128), jnp.float32),
        pltpu.VMEM((9, rows, 16, 128), jnp.float32),
        pltpu.VMEM((5, 16, 128), jnp.float32),
        pltpu.VMEM((5, 16, 128), jnp.float32),
        pltpu.VMEM((2, 5, 16, 128), jnp.float32),
        pltpu.VMEM((2, 5, 16, 128), jnp.float32),
        pltpu.VMEM((2, 2, 16, 128), jnp.float32),
        pltpu.VMEM((2, 2, 16, 128), jnp.float32),
        pltpu.VMEM((3, 5, 16, 128), jnp.float32),
        pltpu.VMEM((3, 5, 16, 128), jnp.float32),
        pltpu.VMEM((5, 80, 128), jnp.float32),
        pltpu.VMEM((5, 80, 128), jnp.float32),
        pltpu.VMEM((2, 5, 8, 128), jnp.float32),
        pltpu.VMEM((2, 5, 8, 128), jnp.float32),
        pltpu.VMEM((16, 128), jnp.float32),
        pltpu.VMEM((16, 128), jnp.float32),
        pltpu.VMEM((128, 128), jnp.float32),
        pltpu.SemaphoreType.DMA((10,)),
        pltpu.SemaphoreType.DMA((22,)),
        pltpu.SemaphoreType.DMA((22,)),
    ]
    return pl.pallas_call(
        kernel,
        out_shape=pltpu.VMEM(populations.shape, jnp.float32),
        in_specs=[pl.BlockSpec(memory_space=pltpu.HBM)] * 6,
        out_specs=pl.BlockSpec(memory_space=pltpu.VMEM),
        scratch_shapes=scratch,
        compiler_params=pltpu.CompilerParams(
            collective_id=0, has_side_effects=True, vmem_limit_bytes=24 << 20
        ),
    )(populations, thermal_noise, relax_rates, plane_shift, fraction_index, plane_speed)


def solution(mesh):
    return jax.shard_map(
        on_device,
        mesh=mesh,
        in_specs=(P(None, "grad", "flow", "vort"), P(None, "grad", "flow", "vort"), P(), P(), P(), P()),
        out_specs=P(None, "grad", "flow", "vort"),
        check_vma=False,
    )
```

time: 177 us -> 41.3 us (0.23)
  the two profiles are of different devices: /device:TPU:199 before, /device:TPU:56 now
where the time goes in v1:
time: 41.3 us; the launch traced here: 41.1 us
  Pallas kernels  35.1 us (85%)
  local copies, waits for them, and re-layouts  5.32 us (13%)
  between operations  0.67 us (2%)
    pallas_call x1, Pallas kernels, on_device(): pl.pallas_call(kernel, out_shape=pltpu.VMEM(populations.shape, jnp.float3...  35.1 us
    unnamed x11, local copies, waits for them, and re-layouts  5.32 us

profile of v1, /device:TPU:56, one launch (start us, length us, event | category | flops | bytes accessed | tf_op | source)
XLA Modules:
  0.0 41.1 jit_solution(8551005144278929464)
XLA Ops:
  0.7 0.0 copy-start
  0.7 1.3 %copy-done = f32[19,8,16,128]{3,2,1,0:T(8,128)S(1)} copy-done((f32[19,8,16,128]{3,2,1,0:T(8,128)S(1)}, f32[19,8,16,128]{3,2,1,0:T(8,128)}, u32[]{:S(2)}) %copy-start) | copy-done | bytes 1245208
  1.9 0.0 copy-start.1
  1.9 1.0 %copy-done.1 = bf16[15,8,16,128]{3,2,1,0:T(8,128)(2,1)S(1)} copy-done((bf16[15,8,16,128]{3,2,1,0:T(8,128)(2,1)S(1)}, bf16[15,8,16,128]{3,2,1,0:T(8,128)(2,1)}, u32[]{:S(2)}) %copy-start.1) | copy-done | bytes 491544
  3.0 0.0 copy-start.2
  3.0 0.7 %copy-done.2 = f32[15]{0:T(128)S(1)} copy-done((f32[15]{0:T(128)S(1)}, f32[15]{0:T(128)}, u32[]{:S(2)}) %copy-start.2) | copy-done | bytes 84
  3.6 0.0 copy-start.3
  3.6 0.7 %copy-done.3 = s32[16]{0:T(128)S(1)} copy-done((s32[16]{0:T(128)S(1)}, s32[16]{0:T(128)}, u32[]{:S(2)}) %copy-start.3) | copy-done | bytes 88
  4.3 0.0 copy-start.4
  4.3 0.7 %copy-done.4 = f32[16]{0:T(128)S(1)} copy-done((f32[16]{0:T(128)S(1)}, f32[16]{0:T(128)}, u32[]{:S(2)}) %copy-start.4) | copy-done | bytes 88
  4.9 35.1 %shard_map.64 = f32[19,8,16,128]{3,2,1,0:T(8,128)S(1)} custom-call(f32[19,8,16,128]{3,2,1,0:T(8,128)S(1)} %copy-done, bf16[15,8,16,128]{3,2,1,0:T(8,128)(2,1)S(1)} %copy-done.1, f32[15]{0:T(128)S(1)} %copy-done.2, s32[16]{0:T(128)S(1)} %copy-done.3, s32[1]{0:T(128)S(6)} %copy.9.frac_hbm, f32[16]{0:T(128)S(1)} %copy-done.4), custom_call_target="tpu_custom_call" | custom-call | tf_op jit(solution)/shard_map/pallas_call | solution.py:385
  40.1 1.0 %copy.8 = f32[19,8,16,128]{3,2,1,0:T(8,128)} copy(f32[19,8,16,128]{3,2,1,0:T(8,128)S(1)} %shard_map.64) | data formatting | bytes 2490368
Async XLA Ops:
  0.7 1.3 %copy-start = (f32[19,8,16,128]{3,2,1,0:T(8,128)S(1)}, f32[19,8,16,128]{3,2,1,0:T(8,128)}, u32[]{:S(2)}) copy-start(f32[19,8,16,128]{3,2,1,0:T(8,128)} %pop_hbm.1) | copy-start | bytes 3735556
  1.9 1.0 %copy-start.1 = (bf16[15,8,16,128]{3,2,1,0:T(8,128)(2,1)S(1)}, bf16[15,8,16,128]{3,2,1,0:T(8,128)(2,1)}, u32[]{:S(2)}) copy-start(bf16[15,8,16,128]{3,2,1,0:T(8,128)(2,1)} %noise_hbm.1) | copy-start | bytes 1474564
  3.0 0.7 %copy-start.2 = (f32[15]{0:T(128)S(1)}, f32[15]{0:T(128)}, u32[]{:S(2)}) copy-start(f32[15]{0:T(128)} %rates_hbm.1) | copy-start | bytes 184
  3.6 0.7 %copy-start.3 = (s32[16]{0:T(128)S(1)}, s32[16]{0:T(128)}, u32[]{:S(2)}) copy-start(s32[16]{0:T(128)} %shift_hbm.1) | copy-start | bytes 196
  4.3 0.7 %copy-start.4 = (f32[16]{0:T(128)S(1)}, f32[16]{0:T(128)}, u32[]{:S(2)}) copy-start(f32[16]{0:T(128)} %speed_hbm.1) | copy-start | bytes 196

commit v2 on v1

--- a/solution.py
+++ b/solution.py
@@ -13,7 +13,7 @@
 MESH = pl.DeviceIdType.MESH
 
 FLOW_UP = (1, 7, 9, 11, 13)
-FLOW_DOWN = (2, 8, 10, 12, 14)
+FLOW_DOWN = (2, 8, 10, 14, 12)
 FLOW_STAY = (0, 3, 4, 5, 6, 15, 16, 17, 18)
 CROSS_UP = (3, 7, 10, 15, 17)
 CROSS_DOWN = (4, 8, 9, 18, 16)
@@ -127,12 +127,12 @@
 
 
 def kernel(
-    pop_hbm, noise_hbm, rates_hbm, shift_hbm, frac_hbm, speed_hbm, out,
-    pv, nv, rates, shift, frac, speed, spread_ref, upad, dpad, stay,
+    pop_hbm, noise_hbm, rates_hbm, shift_hbm, frac, speed_hbm, out,
+    pv, nv, rates, shift, speed, spread_ref, upad, dpad, stay,
     send_up, send_down, first_up, first_down, edge_up, edge_down,
     next_up, next_down, window_up, window_down,
-    flow_out, flow_in, vort_out, vort_in, square,
-    load_sem, send_sem, recv_sem,
+    flow_out, flow_in, corner_in, vort_out, vort_in, square,
+    load_sem, send_sem, recv_sem, ready_sem,
 ):
     g, f, v = lax.axis_index("grad"), lax.axis_index("flow"), lax.axis_index("vort")
     grads, flows, vorts = lax.axis_size("grad"), lax.axis_size("flow"), lax.axis_size("vort")
@@ -144,8 +144,11 @@
         flow_at = lax.rem(side + by_side, 2) * half + lax.rem(x + by_x + half, half)
         return (lax.rem(g + by_g + grads, grads), flow_at, lax.rem(v + by_v + vorts, vorts))
 
-    def along(by_f):
-        return (g, lax.rem(f + by_f + flows, flows), v)
+    def along(by_f, by_v):
+        return (g, lax.rem(f + by_f + flows, flows), lax.rem(v + by_v + vorts, vorts))
+
+    def across(by_g):
+        return [place(by_g, a, 0, c) for a in (1, 0) for c in (0, 1, -1)]
 
     loads = []
 
@@ -160,20 +163,26 @@
     load(pop_hbm.at[:, 0], pv.at[:, 0])
     load(noise_hbm.at[:, 0], nv.at[:, 0])
     load(shift_hbm, shift)
-    load(frac_hbm, frac)
     load(pop_hbm.at[:, pl.ds(1, rows - 2)], pv.at[:, pl.ds(1, rows - 2)])
     load(noise_hbm.at[:, pl.ds(1, rows - 2)], nv.at[:, pl.ds(1, rows - 2)])
 
-    partners = [along(1), along(-1), place(0, 0, 0, 1), place(0, 0, 0, -1)]
+    partners = [along(a, c) for a in (-1, 0, 1) for c in (-1, 0, 1) if a or c]
     partners += [place(0, 0, step, 0) for step in (1, 2, 3)]
-    partners += [place(a, b, 0, c) for a in (1, -1) for b in (0, 1) for c in (0, 1, -1)]
     barrier = pltpu.get_barrier_semaphore()
-    for partner in partners:
-        pl.semaphore_signal(barrier, inc=1, device_id=partner, device_id_type=MESH)
+
+    def greet(semaphore, devices):
+        for device in devices:
+            pl.semaphore_signal(semaphore, inc=1, device_id=device, device_id_type=MESH)
+
+    greet(barrier, partners + across(-1))
+
+    @pl.when(g != grads - 1)
+    def _():
+        greet(barrier, across(1))
 
     copies = []
 
-    def send(source, target, device):
+    def send(source, target, device, started=True):
         number = len(copies)
         copies.append(
             pltpu.make_async_remote_copy(
@@ -185,7 +194,8 @@
                 device_id_type=MESH,
             )
         )
-        copies[-1].start()
+        if started:
+            copies[-1].start()
         return copies[-1]
 
     lane = lax.broadcasted_iota(jnp.int32, (16, 128), 1)
@@ -207,15 +217,13 @@
         for slot, pop in enumerate(FLOW_STAY):
             stay[slot, y] = collided[pop]
 
-    def first_stage(by_g, rows_out, first, edge):
-        return [
-            send(rows_out, first.at[1], place(by_g, 1, 0, 0)),
-            send(rows_out.at[3], edge.at[1, 0], place(by_g, 1, 0, 1)),
-            send(rows_out.at[4], edge.at[1, 1], place(by_g, 1, 0, -1)),
-            send(rows_out, first.at[0], place(by_g, 0, 0, 0)),
-            send(rows_out.at[3], edge.at[0, 0], place(by_g, 0, 0, 1)),
-            send(rows_out.at[4], edge.at[0, 1], place(by_g, 0, 0, -1)),
-        ]
+    def first_stage(by_g, rows_out, first, edge, started):
+        sent = []
+        for which in (1, 0):
+            sent.append(send(rows_out, first.at[which], place(by_g, which, 0, 0), started))
+            sent.append(send(rows_out.at[3], edge.at[which, 0], place(by_g, which, 0, 1), started))
+            sent.append(send(rows_out.at[4], edge.at[which, 1], place(by_g, which, 0, -1), started))
+        return sent
 
     for copy in loads[:4]:
         copy.wait()
@@ -226,20 +234,39 @@
     amount = -speed[lax.rem(g + 1, grads)]
     for slot, pop in enumerate(CROSS_UP):
         send_up[slot] = collided[pop] + jump(pop, density, flow, amount)
-    pl.semaphore_wait(barrier, len(partners))
-    up_first = first_stage(1, send_up, first_up, edge_up)
+
+    @pl.when(g == 0)
+    def _():
+        pl.semaphore_wait(barrier, len(partners) + 6)
+
+    @pl.when(g != 0)
+    def _():
+        pl.semaphore_wait(barrier, len(partners) + 12)
+
+    up_first = first_stage(1, send_up, first_up, edge_up, True)
+
+    @pl.when(g == grads - 1)
+    def _():
+        greet(ready_sem, across(1))
+
     keep(rows - 1, collided)
 
-    for copy in loads[4:8]:
+    for copy in loads[4:7]:
         copy.wait()
     collided, density, flow = collide_row(0)
     amount = speed[g]
     for slot, pop in enumerate(CROSS_DOWN):
         send_down[slot] = collided[pop] + jump(pop, density, flow, amount)
-    down_first = first_stage(-1, send_down, first_down, edge_down)
+    down_first = first_stage(-1, send_down, first_down, edge_down, False)
+
+    @pl.when(g != 0)
+    def _():
+        for copy in down_first:
+            copy.start()
+
     keep(0, collided)
 
-    for copy in loads[8:]:
+    for copy in loads[7:]:
         copy.wait()
 
     def middle(y, carry):
@@ -252,56 +279,35 @@
         for y in range(rows):
             flow_out[0, slot, y : y + 1, :] = upad[slot, y, 23:24, :]
             flow_out[1, slot, y : y + 1, :] = dpad[slot, y, 0:1, :]
-    flow_halo = [
-        send(flow_out.at[0], flow_in.at[0], along(1)),
-        send(flow_out.at[1], flow_in.at[1], along(-1)),
-    ]
-    for copy in flow_halo:
-        copy.wait_recv()
-    for slot in range(5):
-        for y in range(rows):
-            upad[slot, y, 7:8, :] = flow_in[0, slot, y : y + 1, :]
-            dpad[slot, y, 16:17, :] = flow_in[1, slot, y : y + 1, :]
-
-    def shifted(pop, y):
+    halo = []
+    for which, step in enumerate((1, -1)):
+        halo.append(send(flow_out.at[which], flow_in.at[which], along(step, 0)))
+        halo.append(send(flow_out.at[which, 3], corner_in.at[which, 0], along(step, 1)))
+        halo.append(send(flow_out.at[which, 4], corner_in.at[which, 1], along(step, -1)))
+
+    def held(pop):
         if pop in FLOW_UP:
-            return upad[FLOW_UP.index(pop), y, 7:23, :]
+            return upad.at[FLOW_UP.index(pop), :, pl.ds(8, 16), :]
         if pop in FLOW_DOWN:
-            return dpad[FLOW_DOWN.index(pop), y, 1:17, :]
-        return stay[FLOW_STAY.index(pop), y]
+            return dpad.at[FLOW_DOWN.index(pop), :, pl.ds(0, 16), :]
+        return stay.at[FLOW_STAY.index(pop)]
 
     for y in range(rows):
         tile = jnp.zeros((16, 128), jnp.float32)
         for slot, pop in enumerate(VORT_UP):
-            tile = jnp.where(lane == slot, pltpu.roll(shifted(pop, y), slot + 1, 1), tile)
+            tile = jnp.where(lane == slot, pltpu.roll(held(pop)[y], slot + 1, 1), tile)
         for slot, pop in enumerate(VORT_DOWN):
-            tile = jnp.where(lane == 8 + slot, pltpu.roll(shifted(pop, y), 8 + slot, 1), tile)
+            tile = jnp.where(lane == 8 + slot, pltpu.roll(held(pop)[y], 8 + slot, 1), tile)
         square[16 * y : 16 * y + 16, :] = tile
     vort_out[...] = square[...].T[0:16, :]
-    vort_halo = [
-        send(vort_out.at[pl.ds(0, 8)], vort_in.at[pl.ds(0, 8)], place(0, 0, 0, 1)),
-        send(vort_out.at[pl.ds(8, 8)], vort_in.at[pl.ds(8, 8)], place(0, 0, 0, -1)),
-    ]
-
-    def target_rows(pop):
-        step = int(STEPS[pop, 1])
-        return [(y, y + step) for y in range(rows) if 0 <= y + step < rows]
-
-    for pop in range(19):
-        if STEPS[pop, 2] == 0:
-            for y, to in target_rows(pop):
-                out[pop, to] = shifted(pop, y)
-
-    for copy in vort_halo:
-        copy.wait_recv()
-    square[...] = jnp.concatenate([vort_in[...], jnp.zeros((112, 128), jnp.float32)], axis=0).T
-    for slot, (up, down) in enumerate(zip(VORT_UP, VORT_DOWN)):
-        for y, to in target_rows(up):
-            edge = pltpu.roll(square[16 * y : 16 * y + 16, :], (128 - slot) % 128, 1)
-            out[up, to] = jnp.where(lane == 0, edge, pltpu.roll(shifted(up, y), 1, 1))
-        for y, to in target_rows(down):
-            edge = pltpu.roll(square[16 * y : 16 * y + 16, :], 119 - slot, 1)
-            out[down, to] = jnp.where(lane == 127, edge, pltpu.roll(shifted(down, y), 127, 1))
+    halo.append(send(vort_out.at[pl.ds(0, 8)], vort_in.at[pl.ds(0, 8)], along(0, 1)))
+    halo.append(send(vort_out.at[pl.ds(8, 8)], vort_in.at[pl.ds(8, 8)], along(0, -1)))
+
+    @pl.when(g == 0)
+    def _():
+        pl.semaphore_wait(ready_sem, 6)
+        for copy in down_first:
+            copy.start()
 
     far = frac[0].astype(jnp.float32) * (1.0 / FRACS)
 
@@ -343,11 +349,50 @@
 
     down_offset, up_offset = shift[lax.rem(g + 1, grads)], shift[g]
     down_next = second_stage(down_first, first_down, edge_down, next_down, window_down, CROSS_DOWN, down_offset, -1)
+    up_next = second_stage(up_first, first_up, edge_up, next_up, window_up, CROSS_UP, up_offset, 1)
+
+    for copy in halo:
+        copy.wait_recv()
+    square[...] = jnp.concatenate([vort_in[...], jnp.zeros((112, 128), jnp.float32)], axis=0).T
+
+    def target_rows(pop):
+        step = int(STEPS[pop, 1])
+        return [(y, y + step) for y in range(rows) if 0 <= y + step < rows]
+
+    for pop in range(19):
+        for y, to in target_rows(pop):
+            here = held(pop)
+            value = here[y]
+            if pop in VORT_UP:
+                edge = pltpu.roll(square[16 * y : 16 * y + 16, :], (128 - VORT_UP.index(pop)) % 128, 1)
+                value = jnp.where(lane == 0, edge, pltpu.roll(value, 1, 1))
+            elif pop in VORT_DOWN:
+                edge = pltpu.roll(square[16 * y : 16 * y + 16, :], 119 - VORT_DOWN.index(pop), 1)
+                value = jnp.where(lane == 127, edge, pltpu.roll(value, 127, 1))
+            if pop in FLOW_STAY:
+                out[pop, to] = value
+            elif STEPS[pop, 2]:
+                here[y] = value
+    for which in range(2):
+        joined = jnp.where(lane[0:8] == 127, corner_in[which, 0], flow_in[which, 3])
+        flow_in[which, 3] = pltpu.roll(joined, 1, 1)
+        joined = jnp.where(lane[0:8] == 0, corner_in[which, 1], flow_in[which, 4])
+        flow_in[which, 4] = pltpu.roll(joined, 127, 1)
+    for slot, (up, down) in enumerate(zip(FLOW_UP, FLOW_DOWN)):
+        for y, to in target_rows(up):
+            upad[slot, y, 7:8, :] = flow_in[0, slot, y : y + 1, :]
+            out[up, to] = upad[slot, y, 7:23, :]
+        for y, to in target_rows(down):
+            dpad[slot, y, 16:17, :] = flow_in[1, slot, y : y + 1, :]
+            out[down, to] = dpad[slot, y, 1:17, :]
     finish(down_next, window_down, CROSS_DOWN, down_offset, -1, rows - 1)
-    up_next = second_stage(up_first, first_up, edge_up, next_up, window_up, CROSS_UP, up_offset, 1)
     finish(up_next, window_up, CROSS_UP, up_offset, 1, 0)
     for copy in copies:
         copy.wait_send()
+
+
+def pin(whole):
+    return pltpu.with_memory_space_constraint(whole, pltpu.HBM)
 
 
 def on_device(populations, thermal_noise, relax_rates, plane_shift, fraction_index, plane_speed):
@@ -357,7 +402,6 @@
         pltpu.VMEM(thermal_noise.shape, jnp.bfloat16),
         pltpu.SMEM(relax_rates.shape, jnp.float32),
         pltpu.SMEM(plane_shift.shape, jnp.int32),
-        pltpu.SMEM(fraction_index.shape, jnp.int32),
         pltpu.SMEM(plane_speed.shape, jnp.float32),
         pltpu.VMEM((15, 8, 128), jnp.float32),
         pltpu.VMEM((5, rows, 24, 128), jnp.float32),
@@ -375,23 +419,25 @@
         pltpu.VMEM((5, 80, 128), jnp.float32),
         pltpu.VMEM((2, 5, 8, 128), jnp.float32),
         pltpu.VMEM((2, 5, 8, 128), jnp.float32),
+        pltpu.VMEM((2, 2, 8, 128), jnp.float32),
         pltpu.VMEM((16, 128), jnp.float32),
         pltpu.VMEM((16, 128), jnp.float32),
         pltpu.VMEM((128, 128), jnp.float32),
         pltpu.SemaphoreType.DMA((10,)),
-        pltpu.SemaphoreType.DMA((22,)),
-        pltpu.SemaphoreType.DMA((22,)),
+        pltpu.SemaphoreType.DMA((26,)),
+        pltpu.SemaphoreType.DMA((26,)),
+        pltpu.SemaphoreType.REGULAR,
     ]
     return pl.pallas_call(
         kernel,
         out_shape=pltpu.VMEM(populations.shape, jnp.float32),
-        in_specs=[pl.BlockSpec(memory_space=pltpu.HBM)] * 6,
+        in_specs=[pl.BlockSpec(memory_space=pltpu.SMEM if i == 4 else pltpu.HBM) for i in range(6)],
         out_specs=pl.BlockSpec(memory_space=pltpu.VMEM),
         scratch_shapes=scratch,
         compiler_params=pltpu.CompilerParams(
             collective_id=0, has_side_effects=True, vmem_limit_bytes=24 << 20
         ),
-    )(populations, thermal_noise, relax_rates, plane_shift, fraction_index, plane_speed)
+    )(pin(populations), pin(thermal_noise), pin(relax_rates), pin(plane_shift), fraction_index, pin(plane_speed))
 
 
 def solution(mesh):

time: 41.3 us -> 27.5 us (0.67)
  the two profiles are of different devices: /device:TPU:56 before, /device:TPU:8 now
where the time goes in v2:
time: 27.5 us; the launch traced here: 27.3 us
  Pallas kernels  25.6 us (93%)
  local copies, waits for them, and re-layouts  1.04 us (4%)
  between operations  0.66 us (2%)
    pallas_call x1, Pallas kernels, on_device(): pl.pallas_call(kernel, out_shape=pltpu.VMEM(populations.shape, jnp.float3...  25.6 us
    unnamed x1, local copies, waits for them, and re-layouts  1.04 us

profile of v2, /device:TPU:8, one launch (start us, length us, event | category | flops | bytes accessed | tf_op | source)
XLA Modules:
  0.0 27.3 jit_solution(18230572795323337186)
XLA Ops:
  0.7 25.6 %shard_map.64 = f32[19,8,16,128]{3,2,1,0:T(8,128)S(1)} custom-call(f32[19,8,16,128]{3,2,1,0:T(8,128)} %pop_hbm.1, bf16[15,8,16,128]{3,2,1,0:T(8,128)(2,1)} %noise_hbm.1, f32[15]{0:T(128)} %rates_hbm.1, s32[16]{0:T(128)} %shift_hbm.1, s32[1]{0:T(128)S(6)} %copy.9.frac, f32[16]{0:T(128)} %speed_hbm.1), custom_call_target="tpu_custom_call" | custom-call | tf_op jit(solution)/shard_map/pallas_call | solution.py:431
  26.3 1.0 %copy.8 = f32[19,8,16,128]{3,2,1,0:T(8,128)} copy(f32[19,8,16,128]{3,2,1,0:T(8,128)S(1)} %shard_map.64) | data formatting | bytes 2490368

commit v3 on v2

--- a/solution.py
+++ b/solution.py
@@ -129,8 +129,8 @@
 def kernel(
     pop_hbm, noise_hbm, rates_hbm, shift_hbm, frac, speed_hbm, out,
     pv, nv, rates, shift, speed, spread_ref, upad, dpad, stay,
-    send_up, send_down, first_up, first_down, edge_up, edge_down,
-    next_up, next_down, window_up, window_down,
+    send_up, send_down, edge_out_up, edge_out_down, first_up, first_down, late_up, late_down, edge_up, edge_down,
+    next_up, next_down, window_up, window_down, window_late_up, window_late_down,
     flow_out, flow_in, corner_in, vort_out, vort_in, square,
     load_sem, send_sem, recv_sem, ready_sem,
 ):
@@ -166,17 +166,27 @@
     load(pop_hbm.at[:, pl.ds(1, rows - 2)], pv.at[:, pl.ds(1, rows - 2)])
     load(noise_hbm.at[:, pl.ds(1, rows - 2)], nv.at[:, pl.ds(1, rows - 2)])
 
-    partners = [along(a, c) for a in (-1, 0, 1) for c in (-1, 0, 1) if a or c]
-    partners += [place(0, 0, step, 0) for step in (1, 2, 3)]
+    last = grads - 1
+    around = [(a, c) for a in (-1, 0, 1) for c in (-1, 0, 1) if a or c]
     barrier = pltpu.get_barrier_semaphore()
 
     def greet(semaphore, devices):
         for device in devices:
             pl.semaphore_signal(semaphore, inc=1, device_id=device, device_id_type=MESH)
 
-    greet(barrier, partners + across(-1))
-
-    @pl.when(g != grads - 1)
+    def neighbours(slab):
+        places = [along(a, c) for a, c in around] + [place(0, 0, step, 0) for step in (1, 2, 3)]
+        return [(slab, *rest) for _, *rest in places]
+
+    @pl.when(g == last)
+    def _():
+        greet(barrier, across(-1) + neighbours(g - 1))
+
+    @pl.when(g != last)
+    def _():
+        greet(barrier, across(-1) + neighbours(g))
+
+    @pl.when(g < last - 1)
     def _():
         greet(barrier, across(1))
 
@@ -217,13 +227,28 @@
         for slot, pop in enumerate(FLOW_STAY):
             stay[slot, y] = collided[pop]
 
-    def first_stage(by_g, rows_out, first, edge, started):
-        sent = []
+    sub = lax.broadcasted_iota(jnp.int32, (16, 128), 0)
+
+    def turned(column):
+        return jnp.sum(jnp.where(lane == sub, column, 0.0), axis=0, keepdims=True)
+
+    def turned_back(row):
+        return jnp.sum(jnp.where(lane == sub, row, 0.0), axis=1, keepdims=True)
+
+    def first_stage(by_g, rows_out, edge_out, first, edge, started):
+        edge_out[0] = turned(rows_out[3, :, 127:128])
+        edge_out[1] = turned(rows_out[4, :, 0:1])
+        early, late = [], []
         for which in (1, 0):
-            sent.append(send(rows_out, first.at[which], place(by_g, which, 0, 0), started))
-            sent.append(send(rows_out.at[3], edge.at[which, 0], place(by_g, which, 0, 1), started))
-            sent.append(send(rows_out.at[4], edge.at[which, 1], place(by_g, which, 0, -1), started))
-        return sent
+            to = place(by_g, which, 0, 0)
+            early.append(send(rows_out.at[pl.ds(0, 3)], first[0].at[which], to, started))
+        for which in (1, 0):
+            late.append(send(edge_out.at[0], edge.at[which, 0], place(by_g, which, 0, 1), started))
+            late.append(send(edge_out.at[1], edge.at[which, 1], place(by_g, which, 0, -1), started))
+        for which in (1, 0):
+            to = place(by_g, which, 0, 0)
+            late.append(send(rows_out.at[pl.ds(3, 2)], first[1].at[which], to, started))
+        return early, late
 
     for copy in loads[:4]:
         copy.wait()
@@ -235,17 +260,16 @@
     for slot, pop in enumerate(CROSS_UP):
         send_up[slot] = collided[pop] + jump(pop, density, flow, amount)
 
-    @pl.when(g == 0)
-    def _():
-        pl.semaphore_wait(barrier, len(partners) + 6)
-
-    @pl.when(g != 0)
-    def _():
-        pl.semaphore_wait(barrier, len(partners) + 12)
-
-    up_first = first_stage(1, send_up, first_up, edge_up, True)
-
-    @pl.when(g == grads - 1)
+    near = len(around) + 3
+    for when, count in ((g == 0, near + 6), ((g > 0) & (g < last - 1), near + 12), (g == last - 1, 2 * near + 12), (g == last, 6)):
+
+        @pl.when(when)
+        def _(count=count):
+            pl.semaphore_wait(barrier, count)
+
+    up_first = first_stage(1, send_up, edge_out_up, (first_up, late_up), edge_up, True)
+
+    @pl.when(g >= last - 1)
     def _():
         greet(ready_sem, across(1))
 
@@ -257,11 +281,11 @@
     amount = speed[g]
     for slot, pop in enumerate(CROSS_DOWN):
         send_down[slot] = collided[pop] + jump(pop, density, flow, amount)
-    down_first = first_stage(-1, send_down, first_down, edge_down, False)
-
-    @pl.when(g != 0)
-    def _():
-        for copy in down_first:
+    down_first = first_stage(-1, send_down, edge_out_down, (first_down, late_down), edge_down, False)
+
+    @pl.when((g != 0) & (g != last))
+    def _():
+        for copy in down_first[0] + down_first[1]:
             copy.start()
 
     keep(0, collided)
@@ -279,6 +303,13 @@
         for y in range(rows):
             flow_out[0, slot, y : y + 1, :] = upad[slot, y, 23:24, :]
             flow_out[1, slot, y : y + 1, :] = dpad[slot, y, 0:1, :]
+
+    @pl.when(g == last)
+    def _():
+        pl.semaphore_wait(ready_sem, 6)
+        for copy in down_first[0] + down_first[1]:
+            copy.start()
+
     halo = []
     for which, step in enumerate((1, -1)):
         halo.append(send(flow_out.at[which], flow_in.at[which], along(step, 0)))
@@ -306,50 +337,59 @@
     @pl.when(g == 0)
     def _():
         pl.semaphore_wait(ready_sem, 6)
-        for copy in down_first:
+        for copy in down_first[0] + down_first[1]:
             copy.start()
 
     far = frac[0].astype(jnp.float32) * (1.0 / FRACS)
 
-    def second_stage(arrived, first, edge, onward, window, crossing, offset, sign):
+    def second_stage(arrived, slots, first, edge, onward, window, crossing, offset, sign):
         for copy in arrived:
             copy.wait_recv()
-        for which in range(2):
-            first[which, 3] = pltpu.roll(jnp.where(lane == 127, edge[which, 0], first[which, 3]), 1, 1)
-            first[which, 4] = pltpu.roll(jnp.where(lane == 0, edge[which, 1], first[which, 4]), 127, 1)
+        if slots[0] == 3:
+            for which in range(2):
+                upward = pltpu.roll(first[which, 0], 1, 1)
+                first[which, 0] = jnp.where(lane == 0, turned_back(edge[which, 0]), upward)
+                downward = pltpu.roll(first[which, 1], 127, 1)
+                first[which, 1] = jnp.where(lane == 127, turned_back(edge[which, 1]), downward)
         sent = []
+        part = pl.ds(slots[0], len(slots))
         for step in (2, 1, 3, 0):
             to_x = lax.rem(x + sign * step + half, half)
             apart = sign * (to_x - x)
-            for slot, pop in enumerate(crossing):
-                moved = offset + sign * int(STEPS[pop, 0])
+            for at, slot in enumerate(slots):
+                moved = offset + sign * int(STEPS[crossing[slot], 0])
                 chosen = ((apart - ((moved & 127) >> 4)) & 7) >> 2
-                block = first[chosen, slot]
+                block = first[chosen, at]
                 if step:
                     onward[step - 1, slot] = block
                 else:
-                    window[slot, 0:16, :] = block
-                    window[slot, 64:80, :] = block
+                    window[at, 0:16, :] = block
+                    window[at, 64:80, :] = block
             if step:
                 begin = 64 - 16 * step if sign > 0 else 16 * step
-                sent.append(
-                    send(onward.at[step - 1], window.at[:, pl.ds(begin, 16)], place(0, 0, sign * step, 0))
-                )
+                target = window.at[:, pl.ds(begin, 16)]
+                sent.append(send(onward.at[step - 1, part], target, place(0, 0, sign * step, 0)))
         return sent
 
-    def finish(arrived, window, crossing, offset, sign, to):
+    def finish(arrived, slots, window, crossing, offset, sign, to):
         for copy in arrived:
             copy.wait_recv()
-        for slot, pop in enumerate(crossing):
+        for at, slot in enumerate(slots):
+            pop = crossing[slot]
             moved = (offset + sign * int(STEPS[pop, 0])) & 63
             begin = 64 - moved if sign > 0 else moved
-            near_part = window[slot, pl.ds(begin, 16), :]
-            far_part = window[slot, pl.ds(begin - sign, 16), :]
+            near_part = window[at, pl.ds(begin, 16), :]
+            far_part = window[at, pl.ds(begin - sign, 16), :]
             out[pop, to] = (1.0 - far) * near_part + far * far_part
 
     down_offset, up_offset = shift[lax.rem(g + 1, grads)], shift[g]
-    down_next = second_stage(down_first, first_down, edge_down, next_down, window_down, CROSS_DOWN, down_offset, -1)
-    up_next = second_stage(up_first, first_up, edge_up, next_up, window_up, CROSS_UP, up_offset, 1)
+    nexts = []
+    for part, slots in enumerate(((0, 1, 2), (3, 4))):
+        down_rest = ((window_down, window_late_down)[part], CROSS_DOWN, down_offset, -1)
+        up_rest = ((window_up, window_late_up)[part], CROSS_UP, up_offset, 1)
+        down_next = second_stage(down_first[part], slots, (first_down, late_down)[part], edge_down, next_down, *down_rest)
+        up_next = second_stage(up_first[part], slots, (first_up, late_up)[part], edge_up, next_up, *up_rest)
+        nexts.append((slots, down_next, down_rest, up_next, up_rest))
 
     for copy in halo:
         copy.wait_recv()
@@ -385,8 +425,9 @@
         for y, to in target_rows(down):
             dpad[slot, y, 16:17, :] = flow_in[1, slot, y : y + 1, :]
             out[down, to] = dpad[slot, y, 1:17, :]
-    finish(down_next, window_down, CROSS_DOWN, down_offset, -1, rows - 1)
-    finish(up_next, window_up, CROSS_UP, up_offset, 1, 0)
+    for slots, down_next, down_rest, up_next, up_rest in nexts:
+        finish(down_next, slots, *down_rest, rows - 1)
+        finish(up_next, slots, *up_rest, 0)
     for copy in copies:
         copy.wait_send()
 
@@ -409,14 +450,20 @@
         pltpu.VMEM((9, rows, 16, 128), jnp.float32),
         pltpu.VMEM((5, 16, 128), jnp.float32),
         pltpu.VMEM((5, 16, 128), jnp.float32),
-        pltpu.VMEM((2, 5, 16, 128), jnp.float32),
-        pltpu.VMEM((2, 5, 16, 128), jnp.float32),
+        pltpu.VMEM((2, 1, 128), jnp.float32),
+        pltpu.VMEM((2, 1, 128), jnp.float32),
+        pltpu.VMEM((2, 3, 16, 128), jnp.float32),
+        pltpu.VMEM((2, 3, 16, 128), jnp.float32),
         pltpu.VMEM((2, 2, 16, 128), jnp.float32),
         pltpu.VMEM((2, 2, 16, 128), jnp.float32),
+        pltpu.VMEM((2, 2, 1, 128), jnp.float32),
+        pltpu.VMEM((2, 2, 1, 128), jnp.float32),
         pltpu.VMEM((3, 5, 16, 128), jnp.float32),
         pltpu.VMEM((3, 5, 16, 128), jnp.float32),
-        pltpu.VMEM((5, 80, 128), jnp.float32),
-        pltpu.VMEM((5, 80, 128), jnp.float32),
+        pltpu.VMEM((3, 80, 128), jnp.float32),
+        pltpu.VMEM((3, 80, 128), jnp.float32),
+        pltpu.VMEM((2, 80, 128), jnp.float32),
+        pltpu.VMEM((2, 80, 128), jnp.float32),
         pltpu.VMEM((2, 5, 8, 128), jnp.float32),
         pltpu.VMEM((2, 5, 8, 128), jnp.float32),
         pltpu.VMEM((2, 2, 8, 128), jnp.float32),
@@ -424,8 +471,8 @@
         pltpu.VMEM((16, 128), jnp.float32),
         pltpu.VMEM((128, 128), jnp.float32),
         pltpu.SemaphoreType.DMA((10,)),
-        pltpu.SemaphoreType.DMA((26,)),
-        pltpu.SemaphoreType.DMA((26,)),
+        pltpu.SemaphoreType.DMA((36,)),
+        pltpu.SemaphoreType.DMA((36,)),
         pltpu.SemaphoreType.REGULAR,
     ]
     return pl.pallas_call(

time: 27.5 us -> 24.9 us (0.905)
  the two profiles are of different devices: /device:TPU:8 before, /device:TPU:2 now
where the time goes in v3:
time: 24.9 us; the launch traced here: 24.8 us
  Pallas kernels  23.1 us (93%)
  local copies, waits for them, and re-layouts  1.04 us (4%)
  between operations  0.66 us (3%)
    pallas_call x1, Pallas kernels, on_device(): pl.pallas_call(kernel, out_shape=pltpu.VMEM(populations.shape, jnp.float3...  23.1 us
    unnamed x1, local copies, waits for them, and re-layouts  1.04 us

profile of v3, /device:TPU:2, one launch (start us, length us, event | category | flops | bytes accessed | tf_op | source)
XLA Modules:
  0.0 24.8 jit_solution(15797244391169872283)
XLA Ops:
  0.7 23.1 %shard_map.64 = f32[19,8,16,128]{3,2,1,0:T(8,128)S(1)} custom-call(f32[19,8,16,128]{3,2,1,0:T(8,128)} %pop_hbm.1, bf16[15,8,16,128]{3,2,1,0:T(8,128)(2,1)} %noise_hbm.1, f32[15]{0:T(128)} %rates_hbm.1, s32[16]{0:T(128)} %shift_hbm.1, s32[1]{0:T(128)S(6)} %copy.9.frac, f32[16]{0:T(128)} %speed_hbm.1), custom_call_target="tpu_custom_call" | custom-call | tf_op jit(solution)/shard_map/pallas_call | solution.py:478
  23.7 1.0 %copy.8 = f32[19,8,16,128]{3,2,1,0:T(8,128)} copy(f32[19,8,16,128]{3,2,1,0:T(8,128)S(1)} %shard_map.64) | data formatting | bytes 2490368

commit v4 on v3

--- a/solution.py
+++ b/solution.py
@@ -1,4 +1,4 @@
-import functools
+import math
 
 import jax
 import jax.numpy as jnp
@@ -131,7 +131,7 @@
     pv, nv, rates, shift, speed, spread_ref, upad, dpad, stay,
     send_up, send_down, edge_out_up, edge_out_down, first_up, first_down, late_up, late_down, edge_up, edge_down,
     next_up, next_down, window_up, window_down, window_late_up, window_late_down,
-    flow_out, flow_in, corner_in, vort_out, vort_in, square,
+    flow_out, flow_in, corner_in, vort_out, vort_in, square, spare,
     load_sem, send_sem, recv_sem, ready_sem,
 ):
     g, f, v = lax.axis_index("grad"), lax.axis_index("flow"), lax.axis_index("vort")
@@ -154,7 +154,6 @@
 
     def load(source, target):
         loads.append(pltpu.make_async_copy(source, target, load_sem.at[len(loads)]))
-        loads[-1].start()
 
     load(pop_hbm.at[:, rows - 1], pv.at[:, rows - 1])
     load(noise_hbm.at[:, rows - 1], nv.at[:, rows - 1])
@@ -178,35 +177,42 @@
         places = [along(a, c) for a, c in around] + [place(0, 0, step, 0) for step in (1, 2, 3)]
         return [(slab, *rest) for _, *rest in places]
 
-    @pl.when(g == last)
-    def _():
-        greet(barrier, across(-1) + neighbours(g - 1))
+    for copy in loads[:4]:
+        copy.start()
 
     @pl.when(g != last)
     def _():
         greet(barrier, across(-1) + neighbours(g))
+        for copy in loads[4:]:
+            copy.start()
 
     @pl.when(g < last - 1)
     def _():
         greet(barrier, across(1))
 
-    copies = []
-
-    def send(source, target, device, started=True):
-        number = len(copies)
-        copies.append(
-            pltpu.make_async_remote_copy(
-                src_ref=source,
-                dst_ref=target,
-                send_sem=send_sem.at[number],
-                recv_sem=recv_sem.at[number],
-                device_id=device,
-                device_id_type=MESH,
-            )
+    sent_rows, groups = [], {}
+
+    def send(source, target, device, group, started=True):
+        sent_rows.append(math.prod(source.shape) // 128)
+        groups[group] = groups.get(group, 0) + sent_rows[-1]
+        copy = pltpu.make_async_remote_copy(
+            src_ref=source,
+            dst_ref=target,
+            send_sem=send_sem,
+            recv_sem=recv_sem.at[list(groups).index(group)],
+            device_id=device,
+            device_id_type=MESH,
         )
         if started:
-            copies[-1].start()
-        return copies[-1]
+            copy.start()
+        return copy
+
+    def settle(semaphore, count):
+        bytes_of = spare.at[pl.ds(0, count)]
+        pltpu.make_async_copy(bytes_of, bytes_of, semaphore).wait()
+
+    def arrive(group):
+        settle(recv_sem.at[list(groups).index(group)], groups[group])
 
     lane = lax.broadcasted_iota(jnp.int32, (16, 128), 1)
 
@@ -235,20 +241,18 @@
     def turned_back(row):
         return jnp.sum(jnp.where(lane == sub, row, 0.0), axis=1, keepdims=True)
 
-    def first_stage(by_g, rows_out, edge_out, first, edge, started):
+    def first_stage(by_g, rows_out, edge_out, first, edge, name, started):
         edge_out[0] = turned(rows_out[3, :, 127:128])
         edge_out[1] = turned(rows_out[4, :, 0:1])
-        early, late = [], []
+        sent = []
         for which in (1, 0):
             to = place(by_g, which, 0, 0)
-            early.append(send(rows_out.at[pl.ds(0, 3)], first[0].at[which], to, started))
-        for which in (1, 0):
-            late.append(send(edge_out.at[0], edge.at[which, 0], place(by_g, which, 0, 1), started))
-            late.append(send(edge_out.at[1], edge.at[which, 1], place(by_g, which, 0, -1), started))
-        for which in (1, 0):
-            to = place(by_g, which, 0, 0)
-            late.append(send(rows_out.at[pl.ds(3, 2)], first[1].at[which], to, started))
-        return early, late
+            part = name + "0"
+            sent.append(send(rows_out.at[pl.ds(3, 2)], first[0].at[which], to, part, started))
+            sent.append(send(edge_out.at[0], edge.at[which, 0], place(by_g, which, 0, 1), part, started))
+            sent.append(send(edge_out.at[1], edge.at[which, 1], place(by_g, which, 0, -1), part, started))
+            sent.append(send(rows_out.at[pl.ds(0, 3)], first[1].at[which], to, name + "1", started))
+        return sent
 
     for copy in loads[:4]:
         copy.wait()
@@ -267,11 +271,17 @@
         def _(count=count):
             pl.semaphore_wait(barrier, count)
 
-    up_first = first_stage(1, send_up, edge_out_up, (first_up, late_up), edge_up, True)
+    first_stage(1, send_up, edge_out_up, (first_up, late_up), edge_up, "up", True)
 
     @pl.when(g >= last - 1)
     def _():
         greet(ready_sem, across(1))
+
+    @pl.when(g == last)
+    def _():
+        greet(barrier, across(-1) + neighbours(g - 1))
+        for copy in loads[4:]:
+            copy.start()
 
     keep(rows - 1, collided)
 
@@ -281,11 +291,11 @@
     amount = speed[g]
     for slot, pop in enumerate(CROSS_DOWN):
         send_down[slot] = collided[pop] + jump(pop, density, flow, amount)
-    down_first = first_stage(-1, send_down, edge_out_down, (first_down, late_down), edge_down, False)
+    down_first = first_stage(-1, send_down, edge_out_down, (first_down, late_down), edge_down, "down", False)
 
     @pl.when((g != 0) & (g != last))
     def _():
-        for copy in down_first[0] + down_first[1]:
+        for copy in down_first:
             copy.start()
 
     keep(0, collided)
@@ -307,14 +317,13 @@
     @pl.when(g == last)
     def _():
         pl.semaphore_wait(ready_sem, 6)
-        for copy in down_first[0] + down_first[1]:
+        for copy in down_first:
             copy.start()
 
-    halo = []
     for which, step in enumerate((1, -1)):
-        halo.append(send(flow_out.at[which], flow_in.at[which], along(step, 0)))
-        halo.append(send(flow_out.at[which, 3], corner_in.at[which, 0], along(step, 1)))
-        halo.append(send(flow_out.at[which, 4], corner_in.at[which, 1], along(step, -1)))
+        send(flow_out.at[which], flow_in.at[which], along(step, 0), "halo")
+        send(flow_out.at[which, 3], corner_in.at[which, 0], along(step, 1), "halo")
+        send(flow_out.at[which, 4], corner_in.at[which, 1], along(step, -1), "halo")
 
     def held(pop):
         if pop in FLOW_UP:
@@ -331,27 +340,25 @@
             tile = jnp.where(lane == 8 + slot, pltpu.roll(held(pop)[y], 8 + slot, 1), tile)
         square[16 * y : 16 * y + 16, :] = tile
     vort_out[...] = square[...].T[0:16, :]
-    halo.append(send(vort_out.at[pl.ds(0, 8)], vort_in.at[pl.ds(0, 8)], along(0, 1)))
-    halo.append(send(vort_out.at[pl.ds(8, 8)], vort_in.at[pl.ds(8, 8)], along(0, -1)))
+    send(vort_out.at[pl.ds(0, 8)], vort_in.at[pl.ds(0, 8)], along(0, 1), "halo")
+    send(vort_out.at[pl.ds(8, 8)], vort_in.at[pl.ds(8, 8)], along(0, -1), "halo")
 
     @pl.when(g == 0)
     def _():
         pl.semaphore_wait(ready_sem, 6)
-        for copy in down_first[0] + down_first[1]:
+        for copy in down_first:
             copy.start()
 
     far = frac[0].astype(jnp.float32) * (1.0 / FRACS)
 
-    def second_stage(arrived, slots, first, edge, onward, window, crossing, offset, sign):
-        for copy in arrived:
-            copy.wait_recv()
+    def second_stage(name, slots, first, edge, onward, window, crossing, offset, sign):
+        arrive(name)
         if slots[0] == 3:
             for which in range(2):
                 upward = pltpu.roll(first[which, 0], 1, 1)
                 first[which, 0] = jnp.where(lane == 0, turned_back(edge[which, 0]), upward)
                 downward = pltpu.roll(first[which, 1], 127, 1)
                 first[which, 1] = jnp.where(lane == 127, turned_back(edge[which, 1]), downward)
-        sent = []
         part = pl.ds(slots[0], len(slots))
         for step in (2, 1, 3, 0):
             to_x = lax.rem(x + sign * step + half, half)
@@ -368,12 +375,10 @@
             if step:
                 begin = 64 - 16 * step if sign > 0 else 16 * step
                 target = window.at[:, pl.ds(begin, 16)]
-                sent.append(send(onward.at[step - 1, part], target, place(0, 0, sign * step, 0)))
-        return sent
-
-    def finish(arrived, slots, window, crossing, offset, sign, to):
-        for copy in arrived:
-            copy.wait_recv()
+                send(onward.at[step - 1, part], target, place(0, 0, sign * step, 0), name + "next")
+
+    def finish(name, slots, window, crossing, offset, sign, to):
+        arrive(name + "next")
         for at, slot in enumerate(slots):
             pop = crossing[slot]
             moved = (offset + sign * int(STEPS[pop, 0])) & 63
@@ -384,15 +389,15 @@
 
     down_offset, up_offset = shift[lax.rem(g + 1, grads)], shift[g]
     nexts = []
-    for part, slots in enumerate(((0, 1, 2), (3, 4))):
+    for part, slots in enumerate(((3, 4), (0, 1, 2))):
         down_rest = ((window_down, window_late_down)[part], CROSS_DOWN, down_offset, -1)
         up_rest = ((window_up, window_late_up)[part], CROSS_UP, up_offset, 1)
-        down_next = second_stage(down_first[part], slots, (first_down, late_down)[part], edge_down, next_down, *down_rest)
-        up_next = second_stage(up_first[part], slots, (first_up, late_up)[part], edge_up, next_up, *up_rest)
-        nexts.append((slots, down_next, down_rest, up_next, up_rest))
-
-    for copy in halo:
-        copy.wait_recv()
+        part = str(part)
+        second_stage("down" + part, slots, (first_down, late_down)[int(part)], edge_down, next_down, *down_rest)
+        second_stage("up" + part, slots, (first_up, late_up)[int(part)], edge_up, next_up, *up_rest)
+        nexts.append((part, slots, down_rest, up_rest))
+
+    arrive("halo")
     square[...] = jnp.concatenate([vort_in[...], jnp.zeros((112, 128), jnp.float32)], axis=0).T
 
     def target_rows(pop):
@@ -425,11 +430,10 @@
         for y, to in target_rows(down):
             dpad[slot, y, 16:17, :] = flow_in[1, slot, y : y + 1, :]
             out[down, to] = dpad[slot, y, 1:17, :]
-    for slots, down_next, down_rest, up_next, up_rest in nexts:
-        finish(down_next, slots, *down_rest, rows - 1)
-        finish(up_next, slots, *up_rest, 0)
-    for copy in copies:
-        copy.wait_send()
+    for part, slots, down_rest, up_rest in nexts:
+        finish("down" + part, slots, *down_rest, rows - 1)
+        finish("up" + part, slots, *up_rest, 0)
+    settle(send_sem, sum(sent_rows))
 
 
 def pin(whole):
@@ -452,27 +456,28 @@
         pltpu.VMEM((5, 16, 128), jnp.float32),
         pltpu.VMEM((2, 1, 128), jnp.float32),
         pltpu.VMEM((2, 1, 128), jnp.float32),
+        pltpu.VMEM((2, 2, 16, 128), jnp.float32),
+        pltpu.VMEM((2, 2, 16, 128), jnp.float32),
         pltpu.VMEM((2, 3, 16, 128), jnp.float32),
         pltpu.VMEM((2, 3, 16, 128), jnp.float32),
-        pltpu.VMEM((2, 2, 16, 128), jnp.float32),
-        pltpu.VMEM((2, 2, 16, 128), jnp.float32),
         pltpu.VMEM((2, 2, 1, 128), jnp.float32),
         pltpu.VMEM((2, 2, 1, 128), jnp.float32),
         pltpu.VMEM((3, 5, 16, 128), jnp.float32),
         pltpu.VMEM((3, 5, 16, 128), jnp.float32),
+        pltpu.VMEM((2, 80, 128), jnp.float32),
+        pltpu.VMEM((2, 80, 128), jnp.float32),
         pltpu.VMEM((3, 80, 128), jnp.float32),
         pltpu.VMEM((3, 80, 128), jnp.float32),
-        pltpu.VMEM((2, 80, 128), jnp.float32),
-        pltpu.VMEM((2, 80, 128), jnp.float32),
         pltpu.VMEM((2, 5, 8, 128), jnp.float32),
         pltpu.VMEM((2, 5, 8, 128), jnp.float32),
         pltpu.VMEM((2, 2, 8, 128), jnp.float32),
         pltpu.VMEM((16, 128), jnp.float32),
         pltpu.VMEM((16, 128), jnp.float32),
         pltpu.VMEM((128, 128), jnp.float32),
-        pltpu.SemaphoreType.DMA((10,)),
-        pltpu.SemaphoreType.DMA((36,)),
-        pltpu.SemaphoreType.DMA((36,)),
+        pltpu.VMEM((1024, 128), jnp.float32),
+        pltpu.SemaphoreType.DMA((9,)),
+        pltpu.SemaphoreType.DMA,
+        pltpu.SemaphoreType.DMA((9,)),
         pltpu.SemaphoreType.REGULAR,
     ]
     return pl.pallas_call(

time: 24.9 us -> 24 us (0.964)
  Pallas kernels: 23.1 us -> 22.1 us
    pallas_call x1, Pallas kernels: 23.1 us -> 22.1 us  [on_device(): pl.pallas_call(kernel, out_shape=pltpu.VMEM(populations.shape, jnp.float3...]
where the time goes in v4:
time: 24 us; the launch traced here: 23.8 us
  Pallas kernels  22.1 us (92%)
  local copies, waits for them, and re-layouts  1.04 us (4%)
  between operations  0.66 us (3%)
    pallas_call x1, Pallas kernels, on_device(): pl.pallas_call(kernel, out_shape=pltpu.VMEM(populations.shape, jnp.float3...  22.1 us
    unnamed x1, local copies, waits for them, and re-layouts  1.04 us

profile of v4, /device:TPU:2, one launch (start us, length us, event | category | flops | bytes accessed | tf_op | source)
XLA Modules:
  0.0 23.8 jit_solution(4614943591068818774)
XLA Ops:
  0.7 22.1 %shard_map.64 = f32[19,8,16,128]{3,2,1,0:T(8,128)S(1)} custom-call(f32[19,8,16,128]{3,2,1,0:T(8,128)} %pop_hbm.1, bf16[15,8,16,128]{3,2,1,0:T(8,128)(2,1)} %noise_hbm.1, f32[15]{0:T(128)} %rates_hbm.1, s32[16]{0:T(128)} %shift_hbm.1, s32[1]{0:T(128)S(6)} %copy.9.frac, f32[16]{0:T(128)} %speed_hbm.1), custom_call_target="tpu_custom_call" | custom-call | tf_op jit(solution)/shard_map/pallas_call | solution.py:483
  22.8 1.0 %copy.8 = f32[19,8,16,128]{3,2,1,0:T(8,128)} copy(f32[19,8,16,128]{3,2,1,0:T(8,128)S(1)} %shard_map.64) | data formatting | bytes 2490368

commit v5 on v4

--- a/solution.py
+++ b/solution.py
@@ -17,6 +17,7 @@
 FLOW_STAY = (0, 3, 4, 5, 6, 15, 16, 17, 18)
 CROSS_UP = (3, 7, 10, 15, 17)
 CROSS_DOWN = (4, 8, 9, 18, 16)
+PARTS = ((0, 1, 2, 3, 4),)
 VORT_UP = (5, 11, 14, 15, 18)
 VORT_DOWN = (6, 12, 13, 16, 17)
 
@@ -129,8 +130,8 @@
 def kernel(
     pop_hbm, noise_hbm, rates_hbm, shift_hbm, frac, speed_hbm, out,
     pv, nv, rates, shift, speed, spread_ref, upad, dpad, stay,
-    send_up, send_down, edge_out_up, edge_out_down, first_up, first_down, late_up, late_down, edge_up, edge_down,
-    next_up, next_down, window_up, window_down, window_late_up, window_late_down,
+    send_up, send_down, edge_out_up, edge_out_down, first_up, first_down, edge_up, edge_down,
+    next_up, next_down, windows_up, windows_down,
     flow_out, flow_in, corner_in, vort_out, vort_in, square, spare,
     load_sem, send_sem, recv_sem, ready_sem,
 ):
@@ -247,11 +248,12 @@
         sent = []
         for which in (1, 0):
             to = place(by_g, which, 0, 0)
-            part = name + "0"
-            sent.append(send(rows_out.at[pl.ds(3, 2)], first[0].at[which], to, part, started))
-            sent.append(send(edge_out.at[0], edge.at[which, 0], place(by_g, which, 0, 1), part, started))
-            sent.append(send(edge_out.at[1], edge.at[which, 1], place(by_g, which, 0, -1), part, started))
-            sent.append(send(rows_out.at[pl.ds(0, 3)], first[1].at[which], to, name + "1", started))
+            for part, slots in enumerate(PARTS):
+                source = rows_out.at[pl.ds(slots[0], len(slots))]
+                sent.append(send(source, first[part].at[which], to, name + str(part), started))
+                if part == 0:
+                    sent.append(send(edge_out.at[0], edge.at[which, 0], place(by_g, which, 0, 1), name + "0", started))
+                    sent.append(send(edge_out.at[1], edge.at[which, 1], place(by_g, which, 0, -1), name + "0", started))
         return sent
 
     for copy in loads[:4]:
@@ -271,7 +273,7 @@
         def _(count=count):
             pl.semaphore_wait(barrier, count)
 
-    first_stage(1, send_up, edge_out_up, (first_up, late_up), edge_up, "up", True)
+    first_stage(1, send_up, edge_out_up, first_up, edge_up, "up", True)
 
     @pl.when(g >= last - 1)
     def _():
@@ -291,7 +293,7 @@
     amount = speed[g]
     for slot, pop in enumerate(CROSS_DOWN):
         send_down[slot] = collided[pop] + jump(pop, density, flow, amount)
-    down_first = first_stage(-1, send_down, edge_out_down, (first_down, late_down), edge_down, "down", False)
+    down_first = first_stage(-1, send_down, edge_out_down, first_down, edge_down, "down", False)
 
     @pl.when((g != 0) & (g != last))
     def _():
@@ -353,12 +355,13 @@
 
     def second_stage(name, slots, first, edge, onward, window, crossing, offset, sign):
         arrive(name)
-        if slots[0] == 3:
+        if 3 in slots:
+            at3, at4 = slots.index(3), slots.index(4)
             for which in range(2):
-                upward = pltpu.roll(first[which, 0], 1, 1)
-                first[which, 0] = jnp.where(lane == 0, turned_back(edge[which, 0]), upward)
-                downward = pltpu.roll(first[which, 1], 127, 1)
-                first[which, 1] = jnp.where(lane == 127, turned_back(edge[which, 1]), downward)
+                upward = pltpu.roll(first[which, at3], 1, 1)
+                first[which, at3] = jnp.where(lane == 0, turned_back(edge[which, 0]), upward)
+                downward = pltpu.roll(first[which, at4], 127, 1)
+                first[which, at4] = jnp.where(lane == 127, turned_back(edge[which, 1]), downward)
         part = pl.ds(slots[0], len(slots))
         for step in (2, 1, 3, 0):
             to_x = lax.rem(x + sign * step + half, half)
@@ -389,13 +392,12 @@
 
     down_offset, up_offset = shift[lax.rem(g + 1, grads)], shift[g]
     nexts = []
-    for part, slots in enumerate(((3, 4), (0, 1, 2))):
-        down_rest = ((window_down, window_late_down)[part], CROSS_DOWN, down_offset, -1)
-        up_rest = ((window_up, window_late_up)[part], CROSS_UP, up_offset, 1)
-        part = str(part)
-        second_stage("down" + part, slots, (first_down, late_down)[int(part)], edge_down, next_down, *down_rest)
-        second_stage("up" + part, slots, (first_up, late_up)[int(part)], edge_up, next_up, *up_rest)
-        nexts.append((part, slots, down_rest, up_rest))
+    for part, slots in enumerate(PARTS):
+        down_rest = (windows_down[part], CROSS_DOWN, down_offset, -1)
+        up_rest = (windows_up[part], CROSS_UP, up_offset, 1)
+        second_stage("down" + str(part), slots, first_down[part], edge_down, next_down, *down_rest)
+        second_stage("up" + str(part), slots, first_up[part], edge_up, next_up, *up_rest)
+        nexts.append((str(part), slots, down_rest, up_rest))
 
     arrive("halo")
     square[...] = jnp.concatenate([vort_in[...], jnp.zeros((112, 128), jnp.float32)], axis=0).T
@@ -442,6 +444,8 @@
 
 def on_device(populations, thermal_noise, relax_rates, plane_shift, fraction_index, plane_speed):
     rows = populations.shape[1]
+    firsts = [pltpu.VMEM((2, len(slots), 16, 128), jnp.float32) for slots in PARTS]
+    windows = [pltpu.VMEM((len(slots), 80, 128), jnp.float32) for slots in PARTS]
     scratch = [
         pltpu.VMEM(populations.shape, jnp.float32),
         pltpu.VMEM(thermal_noise.shape, jnp.bfloat16),
@@ -456,18 +460,14 @@
         pltpu.VMEM((5, 16, 128), jnp.float32),
         pltpu.VMEM((2, 1, 128), jnp.float32),
         pltpu.VMEM((2, 1, 128), jnp.float32),
-        pltpu.VMEM((2, 2, 16, 128), jnp.float32),
-        pltpu.VMEM((2, 2, 16, 128), jnp.float32),
-        pltpu.VMEM((2, 3, 16, 128), jnp.float32),
-        pltpu.VMEM((2, 3, 16, 128), jnp.float32),
+        firsts,
+        firsts,
         pltpu.VMEM((2, 2, 1, 128), jnp.float32),
         pltpu.VMEM((2, 2, 1, 128), jnp.float32),
         pltpu.VMEM((3, 5, 16, 128), jnp.float32),
         pltpu.VMEM((3, 5, 16, 128), jnp.float32),
-        pltpu.VMEM((2, 80, 128), jnp.float32),
-        pltpu.VMEM((2, 80, 128), jnp.float32),
-        pltpu.VMEM((3, 80, 128), jnp.float32),
-        pltpu.VMEM((3, 80, 128), jnp.float32),
+        windows,
+        windows,
         pltpu.VMEM((2, 5, 8, 128), jnp.float32),
         pltpu.VMEM((2, 5, 8, 128), jnp.float32),
         pltpu.VMEM((2, 2, 8, 128), jnp.float32),

time: 24 us -> 24 us (level)
  the two profiles are of different devices: /device:TPU:2 before, /device:TPU:8 now
where the time goes in v5:
time: 24 us; the launch traced here: 23.9 us
  Pallas kernels  22.2 us (92%)
  local copies, waits for them, and re-layouts  1.04 us (4%)
  between operations  0.66 us (3%)
    pallas_call x1, Pallas kernels, on_device(): pl.pallas_call(kernel, out_shape=pltpu.VMEM(populations.shape, jnp.float3...  22.2 us
    unnamed x1, local copies, waits for them, and re-layouts  1.04 us

profile of v5, /device:TPU:8, one launch (start us, length us, event | category | flops | bytes accessed | tf_op | source)
XLA Modules:
  0.0 23.9 jit_solution(7266917598039245431)
XLA Ops:
  0.7 22.2 %shard_map.64 = f32[19,8,16,128]{3,2,1,0:T(8,128)S(1)} custom-call(f32[19,8,16,128]{3,2,1,0:T(8,128)} %pop_hbm.1, bf16[15,8,16,128]{3,2,1,0:T(8,128)(2,1)} %noise_hbm.1, f32[15]{0:T(128)} %rates_hbm.1, s32[16]{0:T(128)} %shift_hbm.1, s32[1]{0:T(128)S(6)} %copy.9.frac, f32[16]{0:T(128)} %speed_hbm.1), custom_call_target="tpu_custom_call" | custom-call | tf_op jit(solution)/shard_map/pallas_call | solution.py:483
  22.8 1.0 %copy.8 = f32[19,8,16,128]{3,2,1,0:T(8,128)} copy(f32[19,8,16,128]{3,2,1,0:T(8,128)S(1)} %shard_map.64) | data formatting | bytes 2490368

commit v6 on v5

--- a/solution.py
+++ b/solution.py
@@ -156,7 +156,8 @@
     def load(source, target):
         loads.append(pltpu.make_async_copy(source, target, load_sem.at[len(loads)]))
 
-    load(pop_hbm.at[:, rows - 1], pv.at[:, rows - 1])
+    load(pop_hbm.at[pl.ds(0, 10), rows - 1], pv.at[pl.ds(0, 10), rows - 1])
+    load(pop_hbm.at[pl.ds(10, 9), rows - 1], pv.at[pl.ds(10, 9), rows - 1])
     load(noise_hbm.at[:, rows - 1], nv.at[:, rows - 1])
     load(rates_hbm, rates)
     load(speed_hbm, speed)
@@ -178,13 +179,13 @@
         places = [along(a, c) for a, c in around] + [place(0, 0, step, 0) for step in (1, 2, 3)]
         return [(slab, *rest) for _, *rest in places]
 
-    for copy in loads[:4]:
+    for copy in loads[:5]:
         copy.start()
 
     @pl.when(g != last)
     def _():
         greet(barrier, across(-1) + neighbours(g))
-        for copy in loads[4:]:
+        for copy in loads[5:]:
             copy.start()
 
     @pl.when(g < last - 1)
@@ -256,7 +257,7 @@
                     sent.append(send(edge_out.at[1], edge.at[which, 1], place(by_g, which, 0, -1), name + "0", started))
         return sent
 
-    for copy in loads[:4]:
+    for copy in loads[:5]:
         copy.wait()
     for k in range(15):
         scale = THERMAL * float(NORMS[k + 4]) * rates[k] * (2.0 - rates[k])
@@ -282,12 +283,12 @@
     @pl.when(g == last)
     def _():
         greet(barrier, across(-1) + neighbours(g - 1))
-        for copy in loads[4:]:
+        for copy in loads[5:]:
             copy.start()
 
     keep(rows - 1, collided)
 
-    for copy in loads[4:7]:
+    for copy in loads[5:8]:
         copy.wait()
     collided, density, flow = collide_row(0)
     amount = speed[g]
@@ -302,7 +303,7 @@
 
     keep(0, collided)
 
-    for copy in loads[7:]:
+    for copy in loads[8:]:
         copy.wait()
 
     def middle(y, carry):
@@ -475,7 +476,7 @@
         pltpu.VMEM((16, 128), jnp.float32),
         pltpu.VMEM((128, 128), jnp.float32),
         pltpu.VMEM((1024, 128), jnp.float32),
-        pltpu.SemaphoreType.DMA((9,)),
+        pltpu.SemaphoreType.DMA((10,)),
         pltpu.SemaphoreType.DMA,
         pltpu.SemaphoreType.DMA((9,)),
         pltpu.SemaphoreType.REGULAR,

time: 24 us -> 24.1 us (level)
  no operation moved by 1% of the time
where the time goes in v6:
time: 24.1 us; the launch traced here: 23.9 us
  Pallas kernels  22.2 us (92%)
  local copies, waits for them, and re-layouts  1.04 us (4%)
  between operations  0.66 us (3%)
    pallas_call x1, Pallas kernels, on_device(): pl.pallas_call(kernel, out_shape=pltpu.VMEM(populations.shape, jnp.float3...  22.2 us
    unnamed x1, local copies, waits for them, and re-layouts  1.04 us

profile of v6, /device:TPU:8, one launch (start us, length us, event | category | flops | bytes accessed | tf_op | source)
XLA Modules:
  0.0 23.9 jit_solution(17035368740004403884)
XLA Ops:
  0.7 22.2 %shard_map.64 = f32[19,8,16,128]{3,2,1,0:T(8,128)S(1)} custom-call(f32[19,8,16,128]{3,2,1,0:T(8,128)} %pop_hbm.1, bf16[15,8,16,128]{3,2,1,0:T(8,128)(2,1)} %noise_hbm.1, f32[15]{0:T(128)} %rates_hbm.1, s32[16]{0:T(128)} %shift_hbm.1, s32[1]{0:T(128)S(6)} %copy.9.frac, f32[16]{0:T(128)} %speed_hbm.1), custom_call_target="tpu_custom_call" | custom-call | tf_op jit(solution)/shard_map/pallas_call | solution.py:484
  22.9 1.0 %copy.8 = f32[19,8,16,128]{3,2,1,0:T(8,128)} copy(f32[19,8,16,128]{3,2,1,0:T(8,128)S(1)} %shard_map.64) | data formatting | bytes 2490368
